TPU v7x, 512 devices: a whole 4x8x8 slice. The times are simulated.
512 devices in a mesh: span: 32 (over x, y), seq: 16 (over z, core).
Axes of the slice: x: 4, y: 8, z: 8, core: 2. Of those that a mesh axis runs over, the one named last changes fastest.
Arguments:
- q_tok: bfloat16 [65536, 2048], P(('span', 'seq')), may hold values from -300 to 300
- keys: bfloat16 [65536, 512], P(('span', 'seq')), may hold values from -6 to 6
- values: bfloat16 [65536, 512], P(('span', 'seq')), may hold values from -6 to 6
- beacon_q: bfloat16 [8192, 2048], P(('span', 'seq')), may hold values from -15 to 15
- beacon_k: bfloat16 [8192, 512], P(('span', 'seq')), may hold values from -5 to 5
- beacon_v: bfloat16 [8192, 512], P(('span', 'seq')), may hold values from -6 to 6
- beacon_pos: int32 [8192], P('span'), may hold values from 0 to 2047, as said below
- visible: int32 [32, 32], replicated, may hold values 0 or 1
Outputs:
- out_tok: bfloat16 [65536, 2048], P(('span', 'seq'))
- out_beacon: bfloat16 [8192, 2048], P(('span', 'seq'))
Inputs may be any that keep to these rules, and one draw needn't show every extreme that they name: `beacon_pos`: beacon b of a span stands after raw token 8 * b + r of that span, r from 0 to 7; the first beacon of every span at 0, the last at 2047.
All inputs are finite; a program needn't handle non-finite values.
Results may differ from a plain program's by a relative error of at most 0.005.
Values may be sent and summed in bfloat16 or wider, within the bound.
No kernel may reach another device: no remote copies, remote signals or barrier semaphores. Data moves between devices by JAX's collectives and lax.ppermute only.
A program may use at most 64 MiB of HBM per device.

v0:
```python
import functools

import jax
import jax.numpy as jnp
from jax import lax
from jax.experimental import pallas as pl
from jax.experimental.pallas import tpu as pltpu
from jax.sharding import Mesh, PartitionSpec as P

HD = 128
KVH = 4
QH = 16
GROUP = QH // KVH
NX, NY, NZ, NC = 4, 8, 8, 2
TOK = 128
BEA = 16
HEAD_ROWS = TOK + BEA
TILE = GROUP * HEAD_ROWS
TILES = 4
ROWS = TILES * TILE
HALF = 128
SCALE = HD**-0.5 * 1.4426950408889634
LOWEST = -1e30
CHIPS = ("x", "y", "z", "core")
CONTRACT_LAST = (((1,), (1,)), ((), ()))
VMEM = pl.BlockSpec(memory_space=pltpu.VMEM)
SMEM = pl.BlockSpec(memory_space=pltpu.SMEM)
BF16 = jnp.bfloat16
F32 = jnp.float32


def moves(target):
    pairs = []
    for x in range(NX):
        for y in range(NY):
            for z in range(NZ):
                for core in range(NC):
                    to = target(x, y, z, core)
                    if to is not None:
                        tx, ty, tz, tc = to
                        source = ((x * NY + y) * NZ + z) * NC + core
                        pairs.append((source, ((tx * NY + ty) * NZ + tz % NZ) * NC + tc))
    return pairs


def to_head_group(step):
    return moves(lambda x, y, z, core: (x, y, z + 2 * step, core))


def to_later_x(step):
    return moves(lambda x, y, z, core: (x + step, y, z, core) if x + step < NX else None)


OTHER_CORE = moves(lambda x, y, z, core: (x, y, z, 1 - core))
OTHER_PARITY = moves(lambda x, y, z, core: (x, y, z ^ 1, core))


def kernel_call(body, name, out_shape, in_specs, scratch=(), flops=0, byte_count=0):
    return pl.pallas_call(
        body,
        name=name,
        out_shape=out_shape,
        in_specs=in_specs,
        out_specs=jax.tree.map(lambda _: VMEM, out_shape),
        scratch_shapes=list(scratch),
        compiler_params=pltpu.CompilerParams(vmem_limit_bytes=20 * 2**20),
        cost_estimate=pl.CostEstimate(
            flops=flops, bytes_accessed=byte_count, transcendentals=0
        ),
    )


def pack_beacons(k_ref, v_ref, out_ref):
    for z in range(NZ):
        g = z // 2
        piece = jnp.concatenate(
            [k_ref[:, g * HD : (g + 1) * HD], v_ref[:, g * HD : (g + 1) * HD]], axis=1
        )
        for y in range(NY):
            out_ref[y * NZ + z] = piece


def pack_tokens(place, q_ref, k_ref, v_ref, bq_ref, *outs):
    g = place[2] // 2
    for step in range(TILES):
        dest = lax.rem(g + step, KVH)
        out = outs[step]
        for h in range(GROUP):
            column = pl.multiple_of((dest * GROUP + h) * HD, HD)
            out[h * HEAD_ROWS : h * HEAD_ROWS + TOK, :] = q_ref[:, pl.ds(column, HD)]
            out[h * HEAD_ROWS + TOK : (h + 1) * HEAD_ROWS, :] = bq_ref[:, pl.ds(column, HD)]
        column = pl.multiple_of(dest * HD, HD)
        out[TILE : TILE + TOK, :] = k_ref[:, pl.ds(column, HD)]
        out[TILE + TOK : TILE + 2 * TOK, :] = v_ref[:, pl.ds(column, HD)]


def absorb(state, rows, scores, values):
    m_ref, l_ref, a_ref = state
    old = m_ref[rows, :]
    new = jnp.maximum(old, jnp.max(scores, axis=1, keepdims=True))
    weights = jnp.exp2(scores - new[:, :1]).astype(BF16)
    mixed = jnp.dot(weights, values, preferred_element_type=F32)
    factor = jnp.exp2(old - new)
    m_ref[rows, :] = new
    l_ref[rows, :] = l_ref[rows, :] * factor + mixed[:, HD:]
    a_ref[rows, :] = a_ref[rows, :] * factor + mixed[:, :HD]


def score(asked, keys):
    return lax.dot_general(asked, keys, CONTRACT_LAST, preferred_element_type=F32) * SCALE


def list_visible(place, visible, shifts, chosen):
    my_span = place[0] * NY + place[1]
    count = jnp.int32(0)
    for block, shift in enumerate(shifts):
        first = lax.rem(place[0] + NX - shift, NX) * NY
        for y in range(NY):
            earlier = first + y
            usable = (earlier < my_span) & (visible[my_span, earlier] > 0)

            @pl.when(usable)
            def _():
                chosen[count] = block * NY + y

            count = count + usable.astype(jnp.int32)
    return count


def absorb_tile(asked, state, keys, values):
    both = [score(asked[rows, :], keys) for rows in HALVES]
    for rows, scores in zip(HALVES, both):
        absorb(state, rows, scores, values)


def absorb_block(first, size, count, chosen, sources, k_buf, v_buf, run):
    for j in range(size):
        rows = slice(j * 2 * HALF, (j + 1) * 2 * HALF)
        entry = chosen[jnp.minimum(first + j, count - 1)]
        real = first + j < count
        for index, refs in enumerate(sources):

            @pl.when(entry // NY == index)
            def _(refs=refs, rows=rows, entry=entry, real=real):
                span = lax.rem(entry, NY)
                k_buf[rows, :] = jnp.concatenate([r[span, :, :HD] for r in refs], axis=0)

                @pl.when(real)
                def _():
                    v_buf[rows, :HD] = jnp.concatenate([r[span, :, HD:] for r in refs], axis=0)
                    v_buf[rows, HD:] = jnp.ones((2 * HALF, HD), BF16)

                @pl.when(jnp.logical_not(real))
                def _():
                    v_buf[rows, :] = jnp.zeros((2 * HALF, 2 * HD), BF16)

    run(k_buf[: size * 2 * HALF, :], v_buf[: size * 2 * HALF, :])


def absorb_many(count, chosen, sources, k_buf, v_buf, run):
    left = lax.rem(count, 4)
    fold = (left > 0) & (left < 3) & (count > 4)
    blocks = jnp.where(fold, count // 4 - 1, (count + 3) // 4)

    def step(i, _):
        absorb_block(4 * i, 4, count, chosen, sources, k_buf, v_buf, run)
        return 0

    lax.fori_loop(0, blocks, step, 0)

    @pl.when(fold)
    def _():
        absorb_block(4 * blocks, 6, count, chosen, sources, k_buf, v_buf, run)


HALVES = (slice(0, TILE // 2), slice(TILE // 2, TILE))


def over_tiles(q_ref, m_ref, l_ref, a_ref, keys, values):
    def tile_step(tile, _):
        state = (m_ref.at[tile], l_ref.at[tile], a_ref.at[tile])
        absorb_tile(q_ref.at[tile], state, keys, values)
        return 0

    lax.fori_loop(0, TILES, tile_step, 0)


def attend_raw(
    place, bpos, q_ref, kv_o, kv_c, kv_z, kv_zc, mine, other, m_in, l_in, a_in, m_ref, l_ref, a_ref
):
    y, z, core = place[1], place[2], place[3]
    g, parity = z // 2, lax.rem(z, 2)
    pieces = (kv_o, kv_c, kv_z, kv_zc)
    here = parity * 256 + core * 128
    lane = lax.broadcasted_iota(jnp.int32, (1, 512), 1)
    combo = lane // 128
    key_at = ((parity ^ (combo // 2)) * 2 + (core ^ (combo % 2))) * 128 + lane % 128
    blane = lax.broadcasted_iota(jnp.int32, (1, 256), 1)
    brow = blane % 128
    beacon_at = (brow // BEA) * 32 + (core ^ (blane // 128)) * BEA + brow % BEA
    raw_rows = lax.broadcasted_iota(jnp.int32, (TOK, 1), 0) + here
    no_rank = jnp.full((TOK, 1), -1, jnp.int32)
    own_keys = jnp.concatenate([mine[y, :, :HD], other[y, :, :HD]], axis=0)
    own_values = jnp.concatenate([mine[y, :, HD:], other[y, :, HD:]], axis=0)

    def span_tile(source):
        return lax.rem(g - source + KVH, KVH)

    def ask(source, rows):
        tile = span_tile(source)
        kept = [r[tile, :TOK, :] for r in pieces] + [own_keys]
        kept += [r[span_tile(e), :TOK, :] for e in range(source) for r in pieces]
        return score(q_ref[tile, rows, :], jnp.concatenate(kept, axis=0))

    parts = [(source, rows) for source in (3, 2, 1, 0) for rows in HALVES]
    coming = ask(*parts[0])
    for index, (source, rows) in enumerate(parts):
        scores = coming
        if index + 1 < len(parts):
            coming = ask(*parts[index + 1])
        tile = span_tile(source)
        first = source * 64 + parity * 32 + core * BEA
        at = bpos[pl.ds(pl.multiple_of(first, BEA), BEA), :1] - source * 512
        row_at = jnp.concatenate([raw_rows, at] * 2, axis=0)
        rank = first + lax.broadcasted_iota(jnp.int32, (BEA, 1), 0)
        row_rank = jnp.concatenate([no_rank, rank] * 2, axis=0)
        allowed = jnp.concatenate([key_at <= row_at, beacon_at <= row_rank], axis=1)
        near = jnp.where(allowed, scores[:, :768], LOWEST)
        scores = jnp.concatenate([near, scores[:, 768:]], axis=1) if source else near
        kept = [r[tile, TOK:, :] for r in pieces] + [own_values]
        kept += [r[span_tile(e), TOK:, :] for e in range(source) for r in pieces]
        values = jnp.concatenate(kept, axis=0)
        old = m_in[tile, rows, :]
        new = jnp.maximum(old, jnp.max(scores, axis=1, keepdims=True))
        weights = jnp.exp2(scores - new[:, :1]).astype(BF16)
        mixed = jnp.dot(
            weights,
            jnp.concatenate([values, jnp.ones_like(values)], axis=1),
            preferred_element_type=F32,
        )
        factor = jnp.exp2(old - new)
        m_ref[tile, rows, :] = new
        l_ref[tile, rows, :] = l_in[tile, rows, :] * factor + mixed[:, HD:]
        a_ref[tile, rows, :] = a_in[tile, rows, :] * factor + mixed[:, :HD]


def attend_own_x(place, visible, q_ref, mine, other, m_ref, l_ref, a_ref, chosen, k_buf, v_buf):
    m_ref[...] = jnp.full(m_ref.shape, LOWEST, F32)
    l_ref[...] = jnp.zeros(l_ref.shape, F32)
    a_ref[...] = jnp.zeros(a_ref.shape, F32)
    count = list_visible(place, visible, (0,), chosen)
    run = functools.partial(over_tiles, q_ref, m_ref, l_ref, a_ref)
    absorb_many(count, chosen, ((mine, other),), k_buf, v_buf, run)


def attend_next(place, visible, q_ref, mine1, mine3, other1, other3, m_in, l_in, a_in, *rest):
    m_ref, l_ref, a_ref, chosen, k_buf, v_buf = rest
    m_ref[...] = m_in[...]
    l_ref[...] = l_in[...]
    a_ref[...] = a_in[...]
    count = list_visible(place, visible, (1, 3), chosen)
    absorb_many(
        count,
        chosen,
        ((mine1, other1), (mine3, other3)),
        k_buf,
        v_buf,
        functools.partial(over_tiles, q_ref, m_ref, l_ref, a_ref),
    )


def attend_last(tile, place, visible, q_ref, mine, other, m_in, l_in, a_in, out, *rest):
    m_ref, l_ref, a_ref, chosen, k_buf, v_buf = rest
    m_ref[...] = m_in[tile]
    l_ref[...] = l_in[tile]
    a_ref[...] = a_in[tile]
    count = list_visible(place, visible, (2,), chosen)

    run = functools.partial(absorb_tile, q_ref.at[tile], (m_ref, l_ref, a_ref))
    absorb_many(count, chosen, ((mine, other),), k_buf, v_buf, run)
    out[...] = (a_ref[...] / l_ref[...]).astype(BF16)


def unpack_outputs(place, r0, r1, r2, r3, tok_ref, bea_ref):
    g = place[2] // 2
    for step, ref in enumerate((r0, r1, r2, r3)):
        dest = lax.rem(g + step, KVH)
        for h in range(GROUP):
            column = pl.multiple_of((dest * GROUP + h) * HD, HD)
            tok_ref[:, pl.ds(column, HD)] = ref[h * HEAD_ROWS : h * HEAD_ROWS + TOK, :]
            bea_ref[:, pl.ds(column, HD)] = ref[h * HEAD_ROWS + TOK : (h + 1) * HEAD_ROWS, :]


def on_device(q_tok, keys, values, beacon_q, beacon_k, beacon_v, beacon_pos, visible):
    place = jnp.stack([lax.axis_index(a) for a in CHIPS]).astype(jnp.int32)
    bpos = jnp.broadcast_to(beacon_pos[:, None], (256, HD))
    chunks = kernel_call(
        pack_tokens,
        "pack_tokens",
        [jax.ShapeDtypeStruct((TILE + 2 * TOK, HD), BF16)] * TILES,
        [SMEM] + [VMEM] * 4,
        byte_count=1000,
    )(place, q_tok, keys, values, beacon_q)
    got = [chunks[0]] + [
        lax.ppermute(chunks[step], CHIPS, to_head_group(step)) for step in range(1, TILES)
    ]
    to_send = kernel_call(
        pack_beacons,
        "pack_beacons",
        jax.ShapeDtypeStruct((NY * NZ, BEA, 2 * HD), BF16),
        [VMEM] * 2,
        byte_count=1000,
    )(beacon_k, beacon_v)
    arrived = lax.all_to_all(to_send, ("y", "z"), 0, 0, tiled=True)
    block0 = arrived.reshape(NY, HALF, 2 * HD)

    *got, _ = lax.optimization_barrier((*got, block0))
    asked = jnp.stack([piece[:TILE] for piece in got])
    kv_o = jnp.stack([piece[TILE:] for piece in got])
    block0c = lax.ppermute(block0, CHIPS, OTHER_CORE)

    state_shape = [jax.ShapeDtypeStruct((TILES, TILE, HD), F32)] * 3
    scratch = [
        pltpu.SMEM((NX * NY,), jnp.int32),
        pltpu.VMEM((6 * 2 * HALF, HD), BF16),
        pltpu.VMEM((6 * 2 * HALF, 2 * HD), BF16),
    ]
    state = kernel_call(
        attend_own_x,
        "attend_own_x",
        state_shape,
        [SMEM] * 2 + [VMEM] * 3,
        scratch,
        flops=1000,
        byte_count=1000,
    )(place, visible, asked, block0, block0c)
    kv_z = lax.ppermute(kv_o, CHIPS, OTHER_PARITY)
    kv_c = lax.ppermute(kv_o, CHIPS, OTHER_CORE)
    kv_z, _ = lax.optimization_barrier((kv_z, state[1]))
    kv_zc = lax.ppermute(kv_z, CHIPS, OTHER_CORE)
    state = kernel_call(
        attend_raw,
        "attend_raw",
        state_shape,
        [SMEM] + [VMEM] * 11,
        flops=1000,
        byte_count=1000,
    )(place, bpos, asked, kv_o, kv_c, kv_z, kv_zc, block0, block0c, *state)
    arriving = [lax.ppermute(block0, CHIPS, to_later_x(step)) for step in (1, 3, 2)]
    *near, far, _ = lax.optimization_barrier((*arriving, state[1]))
    near_crossed = [lax.ppermute(block, CHIPS, OTHER_CORE) for block in near]
    state = kernel_call(
        attend_next,
        "attend_next",
        state_shape,
        [SMEM] * 2 + [VMEM] * 8,
        scratch,
        flops=1000,
        byte_count=1000,
    )(place, visible, asked, *near, *near_crossed, *state)
    far_crossed = lax.ppermute(far, CHIPS, OTHER_CORE)
    mixed = [None] * TILES
    for tile in (2, 1, 3, 0):
        mixed[tile] = kernel_call(
            functools.partial(attend_last, tile),
            f"attend_last_{tile}",
            jax.ShapeDtypeStruct((TILE, HD), BF16),
            [SMEM] * 2 + [VMEM] * 6,
            [pltpu.VMEM((TILE, HD), F32)] * 3 + scratch,
            flops=1000,
            byte_count=1000,
        )(place, visible, asked, far, far_crossed, *state)
    back = [mixed[0]] + [
        lax.ppermute(mixed[step], CHIPS, to_head_group(-step)) for step in range(1, TILES)
    ]
    return kernel_call(
        unpack_outputs,
        "unpack_outputs",
        [
            jax.ShapeDtypeStruct((TOK, QH * HD), BF16),
            jax.ShapeDtypeStruct((BEA, QH * HD), BF16),
        ],
        [SMEM] + [VMEM] * 4,
        byte_count=1000,
    )(place, *back)


def solution(mesh):
    chips = Mesh(mesh.devices.reshape(NX, NY, NZ, NC), CHIPS)
    rows = P(CHIPS, None)
    return jax.shard_map(
        on_device,
        mesh=chips,
        in_specs=(rows, rows, rows, rows, rows, rows, P(("x", "y")), P()),
        out_specs=(rows, rows),
        check_vma=False,
    )
```

profile of v0, /device:TPU:63, one launch (start us, length us, event | category | flops | bytes accessed | tf_op | source)
XLA Modules:
  0.0 136.0 jit_solution(11365595329778214778)
XLA Ops:
  0.7 0.8 copy-done.5
  2.2 0.8 pack_beacons.1
  3.0 15.6 %all-to-all-start = ((bf16[64,16,256]{2,1,0:T(8,128)(2,1)}), bf16[64,16,256]{2,1,0:T(8,128)(2,1)S(1)}, u32[]{:S(2)}, u32[]{:S(2)}) async-start(bf16[64,16,256]{2,1,0:T(8,128)(2,1)} %pack_beacons.1), calls=%async_computation | async-start | bytes 1048576 | tf_op jit(solution)/shard_map/all_to_all | solution.py:314
  19.5 4.0 %collective-permute-start = (bf16[832,128]{1,0:T(8,128)(2,1)S(1)}, bf16[832,128]{1,0:T(8,128)(2,1)S(1)}, u32[]{:S(2)}, u32[]{:S(2)}) collective-permute-start(bf16[832,128]{1,0:T(8,128)(2,1)S(1)} %get-tuple-element.24), channel_id=1, source_target_pairs={{0,4},{1,5},{2,6},{3,7},{4,8},{5,9},{6,10},{7,11},{8,12},{9,13},{1... | collective-permute-start | bytes 638984 | tf_op jit(solution)/shard_map/ppermute | solution.py:305
  23.5 5.2 %collective-permute-start.1 = (bf16[832,128]{1,0:T(8,128)(2,1)S(1)}, bf16[832,128]{1,0:T(8,128)(2,1)S(1)}, u32[]{:S(2)}, u32[]{:S(2)}) collective-permute-start(bf16[832,128]{1,0:T(8,128)(2,1)S(1)} %get-tuple-element.25), channel_id=1, source_target_pairs={{0,8},{1,9},{2,10},{3,11},{4,12},{5,13},{6,14},{7,15},{8,0},{9,1},... | collective-permute-start | bytes 638984 | tf_op jit(solution)/shard_map/ppermute | solution.py:305
  28.7 5.2 %collective-permute-start.2 = (bf16[832,128]{1,0:T(8,128)(2,1)S(1)}, bf16[832,128]{1,0:T(8,128)(2,1)S(1)}, u32[]{:S(2)}, u32[]{:S(2)}) collective-permute-start(bf16[832,128]{1,0:T(8,128)(2,1)S(1)} %get-tuple-element.26), channel_id=1, source_target_pairs={{0,12},{1,13},{2,14},{3,15},{4,0},{5,1},{6,2},{7,3},{8,4},{9,5},{1... | collective-permute-start | bytes 638984 | tf_op jit(solution)/shard_map/ppermute | solution.py:305
  33.9 1.5 %all-to-all-done = bf16[64,16,256]{2,1,0:T(8,128)(2,1)S(1)} async-done(((bf16[64,16,256]{2,1,0:T(8,128)(2,1)}), bf16[64,16,256]{2,1,0:T(8,128)(2,1)S(1)}, u32[]{:S(2)}, u32[]{:S(2)}) %all-to-all-start) | async-done | bytes 524320 | tf_op jit(solution)/shard_map/all_to_all | solution.py:314
  35.5 4.2 %collective-permute-start.8 = (bf16[8,128,256]{2,1,0:T(8,128)(2,1)S(1)}, bf16[8,128,256]{2,1,0:T(8,128)(2,1)S(1)}, u32[]{:S(2)}, u32[]{:S(2)}) collective-permute-start(bf16[8,128,256]{2,1,0:T(8,128)(2,1)S(1)} %bitcast.21), channel_id=1, source_target_pairs={{0,1},{1,0},{2,3},{3,2},{4,5},{5,4},{6,7},{7,6},{8,9},{9,8},{10,11... | collective-permute-start | bytes 1572872 | tf_op jit(solution)/shard_map/ppermute | solution.py:320
  39.7 1.3 collective-permute-start.3
  41.0 1.0 collective-permute-done
  42.0 1.3 collective-permute-start.4
  43.3 10.8 %collective-permute-done.1 = bf16[832,128]{1,0:T(8,128)(2,1)S(1)} collective-permute-done((bf16[832,128]{1,0:T(8,128)(2,1)S(1)}, bf16[832,128]{1,0:T(8,128)(2,1)S(1)}, u32[]{:S(2)}, u32[]{:S(2)}) %collective-permute-start.1) | collective-permute-done | bytes 213024 | tf_op jit(solution)/shard_map/ppermute | solution.py:305
  54.1 1.3 collective-permute-start.5
  55.5 1.9 %collective-permute-start.7 = (bf16[4,256,128]{2,1,0:T(8,128)(2,1)S(1)}, bf16[4,256,128]{2,1,0:T(8,128)(2,1)S(1)}, u32[]{:S(2)}, u32[]{:S(2)}) collective-permute-start(bf16[4,256,128]{2,1,0:T(8,128)(2,1)S(1)} %pad_maximum_fusion.1.kv_o), channel_id=1, source_target_pairs={{0,2},{1,3},{2,0},{3,1},{4,6},{5,7},{6,4},{7,5},{8,10},{9,11},{10,... | collective-permute-start | bytes 786440 | tf_op jit(solution)/shard_map/ppermute | solution.py:337
  57.6 2.7 %collective-permute-start.6 = (bf16[4,256,128]{2,1,0:T(8,128)(2,1)S(1)}, bf16[4,256,128]{2,1,0:T(8,128)(2,1)S(1)}, u32[]{:S(2)}, u32[]{:S(2)}) collective-permute-start(bf16[4,256,128]{2,1,0:T(8,128)(2,1)S(1)} %pad_maximum_fusion.1.kv_o), channel_id=1, source_target_pairs={{0,1},{1,0},{2,3},{3,2},{4,5},{5,4},{6,7},{7,6},{8,9},{9,8},{10,11... | collective-permute-start | bytes 786440 | tf_op jit(solution)/shard_map/ppermute | solution.py:338
  60.3 10.6 %attend_own_x.1 = (f32[4,576,128]{2,1,0:T(8,128)S(1)}, f32[4,576,128]{2,1,0:T(8,128)S(1)}, f32[4,576,128]{2,1,0:T(8,128)S(1)}) custom-call(s32[4]{0:T(128)S(1)} %pad_add_fusion.place, s32[32,32]{1,0:T(8,128)S(1)} %copy-done, bf16[4,576,128]{2,1,0:T(8,128)(2,1)S(1)} %pad_maximum_fusion.q_ref, bf16[8,128,256]{2,1,0:T(8,128)(2,1)S(1)} %bitcast.25, ...), custom_call_target="tpu_custom_call" | custom-call | flops 1000 | bytes 1000 | tf_op jit(solution)/shard_map/attend_own_x/pallas_call | solution.py:328
  70.9 1.9 %collective-permute-start.9 = (bf16[4,256,128]{2,1,0:T(8,128)(2,1)S(1)}, bf16[4,256,128]{2,1,0:T(8,128)(2,1)S(1)}, u32[]{:S(2)}, u32[]{:S(2)}) collective-permute-start(bf16[4,256,128]{2,1,0:T(8,128)(2,1)S(1)} %collective-permute-done.7.kv_z), channel_id=1, source_target_pairs={{0,1},{1,0},{2,3},{3,2},{4,5},{5,4},{6,7},{7,6},{8,9},{9,8},{10,11... | collective-permute-start | bytes 786440 | tf_op jit(solution)/shard_map/ppermute | solution.py:340
  72.9 1.5 %collective-permute-done.9.kv_zc = bf16[4,256,128]{2,1,0:T(8,128)(2,1)S(1)} collective-permute-done((bf16[4,256,128]{2,1,0:T(8,128)(2,1)S(1)}, bf16[4,256,128]{2,1,0:T(8,128)(2,1)S(1)}, u32[]{:S(2)}, u32[]{:S(2)}) %collective-permute-start.9) | collective-permute-done | bytes 262176 | tf_op jit(solution)/shard_map/ppermute | solution.py:340
  74.5 5.9 %attend_raw.1 = (f32[4,576,128]{2,1,0:T(8,128)S(1)}, f32[4,576,128]{2,1,0:T(8,128)S(1)}, f32[4,576,128]{2,1,0:T(8,128)S(1)}) custom-call(s32[4]{0:T(128)S(1)} %pad_add_fusion.place, s32[256,128]{1,0:T(8,128)S(1)} %broadcast_in_dim.2.bpos, bf16[4,576,128]{2,1,0:T(8,128)(2,1)S(1)} %pad_maximum_fusion.q_ref, bf16[4,256,128]{2,1,0:T(8,128)(2,1)S(1)} %pad_maximum_fusion.1.kv_o, ...), custom_call_target="tpu_custom_call" | custom-call | flops 1000 | bytes 1000 | tf_op jit(solution)/shard_map/attend_raw/pallas_call | solution.py:341
  80.5 2.0 %collective-permute-start.11 = (bf16[8,128,256]{2,1,0:T(8,128)(2,1)S(1)}, bf16[8,128,256]{2,1,0:T(8,128)(2,1)S(1)}, u32[]{:S(2)}, u32[]{:S(2)}) collective-permute-start(bf16[8,128,256]{2,1,0:T(8,128)(2,1)S(1)} %collective-permute-done.3.mine1), channel_id=1, source_target_pairs={{0,1},{1,0},{2,3},{3,2},{4,5},{5,4},{6,7},{7,6},{8,9},{9,8},{10,11... | collective-permute-start | bytes 1572872 | tf_op jit(solution)/shard_map/ppermute | solution.py:351
  82.5 2.3 %collective-permute-start.12 = (bf16[8,128,256]{2,1,0:T(8,128)(2,1)S(1)}, bf16[8,128,256]{2,1,0:T(8,128)(2,1)S(1)}, u32[]{:S(2)}, u32[]{:S(2)}) collective-permute-start(bf16[8,128,256]{2,1,0:T(8,128)(2,1)S(1)} %collective-permute-done.4.mine3), channel_id=1, source_target_pairs={{0,1},{1,0},{2,3},{3,2},{4,5},{5,4},{6,7},{7,6},{8,9},{9,8},{10,11... | collective-permute-start | bytes 1572872 | tf_op jit(solution)/shard_map/ppermute | solution.py:351
  84.8 2.0 %collective-permute-start.10 = (bf16[8,128,256]{2,1,0:T(8,128)(2,1)S(1)}, bf16[8,128,256]{2,1,0:T(8,128)(2,1)S(1)}, u32[]{:S(2)}, u32[]{:S(2)}) collective-permute-start(bf16[8,128,256]{2,1,0:T(8,128)(2,1)S(1)} %collective-permute-done.5.mine), channel_id=1, source_target_pairs={{0,1},{1,0},{2,3},{3,2},{4,5},{5,4},{6,7},{7,6},{8,9},{9,8},{10,11... | collective-permute-start | bytes 1572872 | tf_op jit(solution)/shard_map/ppermute | solution.py:361
  86.9 15.7 %attend_next.1 = (f32[4,576,128]{2,1,0:T(8,128)S(1)}, f32[4,576,128]{2,1,0:T(8,128)S(1)}, f32[4,576,128]{2,1,0:T(8,128)S(1)}) custom-call(s32[4]{0:T(128)S(1)} %pad_add_fusion.place, s32[32,32]{1,0:T(8,128)S(1)} %copy-done, bf16[4,576,128]{2,1,0:T(8,128)(2,1)S(1)} %pad_maximum_fusion.q_ref, bf16[8,128,256]{2,1,0:T(8,128)(2,1)S(1)} %collective-permute-done.3.mine1, ...), custom_call_target="tpu_custom_call" | custom-call | flops 1000 | bytes 1000 | tf_op jit(solution)/shard_map/attend_next/pallas_call | solution.py:352
  102.6 3.5 %attend_last_3.1 = bf16[576,128]{1,0:T(8,128)(2,1)S(1)} custom-call(s32[4]{0:T(128)S(1)} %pad_add_fusion.place, s32[32,32]{1,0:T(8,128)S(1)} %copy-done, bf16[4,576,128]{2,1,0:T(8,128)(2,1)S(1)} %pad_maximum_fusion.q_ref, bf16[8,128,256]{2,1,0:T(8,128)(2,1)S(1)} %collective-permute-done.5.mine, bf16[8,128,256]{2,1,0:T(8,128)(2,1)S(1)} %collective-permute-done.10.other, ...), custom_call_target="tpu_custom_call" | custom-call | flops 1000 | bytes 1000 | tf_op jit(solution)/shard_map/attend_last_3/pallas_call | solution.py:364
  106.2 2.2 %collective-permute-start.15 = (bf16[576,128]{1,0:T(8,128)(2,1)S(1)}, bf16[576,128]{1,0:T(8,128)(2,1)S(1)}, u32[]{:S(2)}, u32[]{:S(2)}) collective-permute-start(bf16[576,128]{1,0:T(8,128)(2,1)S(1)} %attend_last_3.1), channel_id=1, source_target_pairs={{0,4},{1,5},{2,6},{3,7},{4,8},{5,9},{6,10},{7,11},{8,12},{9,13},{1... | collective-permute-start | bytes 442376 | tf_op jit(solution)/shard_map/ppermute | solution.py:374
  108.4 3.5 %attend_last_2.1 = bf16[576,128]{1,0:T(8,128)(2,1)S(1)} custom-call(s32[4]{0:T(128)S(1)} %pad_add_fusion.place, s32[32,32]{1,0:T(8,128)S(1)} %copy-done, bf16[4,576,128]{2,1,0:T(8,128)(2,1)S(1)} %pad_maximum_fusion.q_ref, bf16[8,128,256]{2,1,0:T(8,128)(2,1)S(1)} %collective-permute-done.5.mine, bf16[8,128,256]{2,1,0:T(8,128)(2,1)S(1)} %collective-permute-done.10.other, ...), custom_call_target="tpu_custom_call" | custom-call | flops 1000 | bytes 1000 | tf_op jit(solution)/shard_map/attend_last_2/pallas_call | solution.py:364
  111.9 4.5 %collective-permute-start.14 = (bf16[576,128]{1,0:T(8,128)(2,1)S(1)}, bf16[576,128]{1,0:T(8,128)(2,1)S(1)}, u32[]{:S(2)}, u32[]{:S(2)}) collective-permute-start(bf16[576,128]{1,0:T(8,128)(2,1)S(1)} %attend_last_2.1), channel_id=1, source_target_pairs={{0,8},{1,9},{2,10},{3,11},{4,12},{5,13},{6,14},{7,15},{8,0},{9,1},... | collective-permute-start | bytes 442376 | tf_op jit(solution)/shard_map/ppermute | solution.py:374
  116.4 3.8 %attend_last_1.1 = bf16[576,128]{1,0:T(8,128)(2,1)S(1)} custom-call(s32[4]{0:T(128)S(1)} %pad_add_fusion.place, s32[32,32]{1,0:T(8,128)S(1)} %copy-done, bf16[4,576,128]{2,1,0:T(8,128)(2,1)S(1)} %pad_maximum_fusion.q_ref, bf16[8,128,256]{2,1,0:T(8,128)(2,1)S(1)} %collective-permute-done.5.mine, bf16[8,128,256]{2,1,0:T(8,128)(2,1)S(1)} %collective-permute-done.10.other, ...), custom_call_target="tpu_custom_call" | custom-call | flops 1000 | bytes 1000 | tf_op jit(solution)/shard_map/attend_last_1/pallas_call | solution.py:364
  120.2 5.5 %collective-permute-start.13 = (bf16[576,128]{1,0:T(8,128)(2,1)S(1)}, bf16[576,128]{1,0:T(8,128)(2,1)S(1)}, u32[]{:S(2)}, u32[]{:S(2)}) collective-permute-start(bf16[576,128]{1,0:T(8,128)(2,1)S(1)} %attend_last_1.1), channel_id=1, source_target_pairs={{0,12},{1,13},{2,14},{3,15},{4,0},{5,1},{6,2},{7,3},{8,4},{9,5},{1... | collective-permute-start | bytes 442376 | tf_op jit(solution)/shard_map/ppermute | solution.py:374
  125.6 3.5 %attend_last_0.1.r0 = bf16[576,128]{1,0:T(8,128)(2,1)S(1)} custom-call(s32[4]{0:T(128)S(1)} %pad_add_fusion.place, s32[32,32]{1,0:T(8,128)S(1)} %copy-done, bf16[4,576,128]{2,1,0:T(8,128)(2,1)S(1)} %pad_maximum_fusion.q_ref, bf16[8,128,256]{2,1,0:T(8,128)(2,1)S(1)} %collective-permute-done.5.mine, bf16[8,128,256]{2,1,0:T(8,128)(2,1)S(1)} %collective-permute-done.10.other, ...), custom_call_target="tpu_custom_call" | custom-call | flops 1000 | bytes 1000 | tf_op jit(solution)/shard_map/attend_last_0/pallas_call | solution.py:364
  129.2 5.2 %collective-permute-done.13.r1 = bf16[576,128]{1,0:T(8,128)(2,1)S(1)} collective-permute-done((bf16[576,128]{1,0:T(8,128)(2,1)S(1)}, bf16[576,128]{1,0:T(8,128)(2,1)S(1)}, u32[]{:S(2)}, u32[]{:S(2)}) %collective-permute-start.13) | collective-permute-done | bytes 147488 | tf_op jit(solution)/shard_map/ppermute | solution.py:374
  134.5 1.5 %unpack_outputs.1 = (bf16[128,2048]{1,0:T(8,128)(2,1)}, bf16[16,2048]{1,0:T(8,128)(2,1)}) custom-call(s32[4]{0:T(128)S(1)} %pad_add_fusion.place, bf16[576,128]{1,0:T(8,128)(2,1)S(1)} %attend_last_0.1.r0, bf16[576,128]{1,0:T(8,128)(2,1)S(1)} %collective-permute-done.13.r1, bf16[576,128]{1,0:T(8,128)(2,1)S(1)} %collective-permute-done.14.r2, ...), custom_call_target="tpu_custom_call" | custom-call | bytes 1000 | tf_op jit(solution)/shard_map/unpack_outputs/pallas_call | solution.py:376
  (36 shorter events, 1.9 us)
Async XLA Ops:
  0.6 18.1 %copy-start.3 = (bf16[128,512]{1,0:T(8,128)(2,1)S(1)}, bf16[128,512]{1,0:T(8,128)(2,1)}, u32[]{:S(2)}) copy-start(bf16[128,512]{1,0:T(8,128)(2,1)} %v_ref.2) | copy-start | bytes 393220
  0.6 18.1 %copy-start.4 = (bf16[16,2048]{1,0:T(8,128)(2,1)S(1)}, bf16[16,2048]{1,0:T(8,128)(2,1)}, u32[]{:S(2)}) copy-start(bf16[16,2048]{1,0:T(8,128)(2,1)} %bq_ref.1) | copy-start | bytes 196612
  0.7 18.1 %copy-start.1 = (bf16[128,2048]{1,0:T(8,128)(2,1)S(1)}, bf16[128,2048]{1,0:T(8,128)(2,1)}, u32[]{:S(2)}) copy-start(bf16[128,2048]{1,0:T(8,128)(2,1)} %q_ref.1) | copy-start | bytes 1572868
  0.7 18.1 %copy-start.2 = (bf16[128,512]{1,0:T(8,128)(2,1)S(1)}, bf16[128,512]{1,0:T(8,128)(2,1)}, u32[]{:S(2)}) copy-start(bf16[128,512]{1,0:T(8,128)(2,1)} %k_ref.2) | copy-start | bytes 393220
  0.7 0.8 copy-start.5
  1.5 0.7 copy-start.6
  3.0 32.5 %all-to-all-start = ((bf16[64,16,256]{2,1,0:T(8,128)(2,1)}), bf16[64,16,256]{2,1,0:T(8,128)(2,1)S(1)}, u32[]{:S(2)}, u32[]{:S(2)}) async-start(bf16[64,16,256]{2,1,0:T(8,128)(2,1)} %pack_beacons.1), calls=%async_computation | async-start | bytes 1048576 | tf_op jit(solution)/shard_map/all_to_all | solution.py:314
  19.5 22.5 %collective-permute-start = (bf16[832,128]{1,0:T(8,128)(2,1)S(1)}, bf16[832,128]{1,0:T(8,128)(2,1)S(1)}, u32[]{:S(2)}, u32[]{:S(2)}) collective-permute-start(bf16[832,128]{1,0:T(8,128)(2,1)S(1)} %get-tuple-element.24), channel_id=1, source_target_pairs={{0,4},{1,5},{2,6},{3,7},{4,8},{5,9},{6,10},{7,11},{8,12},{9,13},{1... | collective-permute-start | bytes 638984 | tf_op jit(solution)/shard_map/ppermute | solution.py:305
  23.5 30.6 %collective-permute-start.1 = (bf16[832,128]{1,0:T(8,128)(2,1)S(1)}, bf16[832,128]{1,0:T(8,128)(2,1)S(1)}, u32[]{:S(2)}, u32[]{:S(2)}) collective-permute-start(bf16[832,128]{1,0:T(8,128)(2,1)S(1)} %get-tuple-element.25), channel_id=1, source_target_pairs={{0,8},{1,9},{2,10},{3,11},{4,12},{5,13},{6,14},{7,15},{8,0},{9,1},... | collective-permute-start | bytes 638984 | tf_op jit(solution)/shard_map/ppermute | solution.py:305
  28.7 26.6 %collective-permute-start.2 = (bf16[832,128]{1,0:T(8,128)(2,1)S(1)}, bf16[832,128]{1,0:T(8,128)(2,1)S(1)}, u32[]{:S(2)}, u32[]{:S(2)}) collective-permute-start(bf16[832,128]{1,0:T(8,128)(2,1)S(1)} %get-tuple-element.26), channel_id=1, source_target_pairs={{0,12},{1,13},{2,14},{3,15},{4,0},{5,1},{6,2},{7,3},{8,4},{9,5},{1... | collective-permute-start | bytes 638984 | tf_op jit(solution)/shard_map/ppermute | solution.py:305
  35.5 22.1 %collective-permute-start.8 = (bf16[8,128,256]{2,1,0:T(8,128)(2,1)S(1)}, bf16[8,128,256]{2,1,0:T(8,128)(2,1)S(1)}, u32[]{:S(2)}, u32[]{:S(2)}) collective-permute-start(bf16[8,128,256]{2,1,0:T(8,128)(2,1)S(1)} %bitcast.21), channel_id=1, source_target_pairs={{0,1},{1,0},{2,3},{3,2},{4,5},{5,4},{6,7},{7,6},{8,9},{9,8},{10,11... | collective-permute-start | bytes 1572872 | tf_op jit(solution)/shard_map/ppermute | solution.py:320
  39.7 40.7 %collective-permute-start.3 = (bf16[8,128,256]{2,1,0:T(8,128)(2,1)S(1)}, bf16[8,128,256]{2,1,0:T(8,128)(2,1)S(1)}, u32[]{:S(2)}, u32[]{:S(2)}) collective-permute-start(bf16[8,128,256]{2,1,0:T(8,128)(2,1)S(1)} %bitcast.22), channel_id=1, source_target_pairs={{0,128},{1,129},{2,130},{3,131},{4,132},{5,133},{6,134},{7,135},{8... | collective-permute-start | bytes 1572872 | tf_op jit(solution)/shard_map/ppermute | solution.py:349
  42.0 38.5 %collective-permute-start.4 = (bf16[8,128,256]{2,1,0:T(8,128)(2,1)S(1)}, bf16[8,128,256]{2,1,0:T(8,128)(2,1)S(1)}, u32[]{:S(2)}, u32[]{:S(2)}) collective-permute-start(bf16[8,128,256]{2,1,0:T(8,128)(2,1)S(1)} %bitcast.23), channel_id=1, source_target_pairs={{0,384},{1,385},{2,386},{3,387},{4,388},{5,389},{6,390},{7,391},{8... | collective-permute-start | bytes 1572872 | tf_op jit(solution)/shard_map/ppermute | solution.py:349
  54.1 26.4 %collective-permute-start.5 = (bf16[8,128,256]{2,1,0:T(8,128)(2,1)S(1)}, bf16[8,128,256]{2,1,0:T(8,128)(2,1)S(1)}, u32[]{:S(2)}, u32[]{:S(2)}) collective-permute-start(bf16[8,128,256]{2,1,0:T(8,128)(2,1)S(1)} %bitcast.24), channel_id=1, source_target_pairs={{0,256},{1,257},{2,258},{3,259},{4,260},{5,261},{6,262},{7,263},{8... | collective-permute-start | bytes 1572872 | tf_op jit(solution)/shard_map/ppermute | solution.py:349
  55.5 4.8 %copy-start = (s32[32,32]{1,0:T(8,128)S(1)}, s32[32,32]{1,0:T(8,128)}, u32[]{:S(2)}) copy-start(s32[32,32]{1,0:T(8,128)} %visible.11) | copy-start | bytes 12292
  55.5 15.5 %collective-permute-start.7 = (bf16[4,256,128]{2,1,0:T(8,128)(2,1)S(1)}, bf16[4,256,128]{2,1,0:T(8,128)(2,1)S(1)}, u32[]{:S(2)}, u32[]{:S(2)}) collective-permute-start(bf16[4,256,128]{2,1,0:T(8,128)(2,1)S(1)} %pad_maximum_fusion.1.kv_o), channel_id=1, source_target_pairs={{0,2},{1,3},{2,0},{3,1},{4,6},{5,7},{6,4},{7,5},{8,10},{9,11},{10,... | collective-permute-start | bytes 786440 | tf_op jit(solution)/shard_map/ppermute | solution.py:337
  57.5 16.9 %copy-start.7 = (s32[256]{0:T(256)S(1)}, s32[256]{0:T(256)}, u32[]{:S(2)}) copy-start(s32[256]{0:T(256)} %param.14) | copy-start | bytes 3076
  57.6 15.3 %collective-permute-start.6 = (bf16[4,256,128]{2,1,0:T(8,128)(2,1)S(1)}, bf16[4,256,128]{2,1,0:T(8,128)(2,1)S(1)}, u32[]{:S(2)}, u32[]{:S(2)}) collective-permute-start(bf16[4,256,128]{2,1,0:T(8,128)(2,1)S(1)} %pad_maximum_fusion.1.kv_o), channel_id=1, source_target_pairs={{0,1},{1,0},{2,3},{3,2},{4,5},{5,4},{6,7},{7,6},{8,9},{9,8},{10,11... | collective-permute-start | bytes 786440 | tf_op jit(solution)/shard_map/ppermute | solution.py:338
  70.9 3.4 %collective-permute-start.9 = (bf16[4,256,128]{2,1,0:T(8,128)(2,1)S(1)}, bf16[4,256,128]{2,1,0:T(8,128)(2,1)S(1)}, u32[]{:S(2)}, u32[]{:S(2)}) collective-permute-start(bf16[4,256,128]{2,1,0:T(8,128)(2,1)S(1)} %collective-permute-done.7.kv_z), channel_id=1, source_target_pairs={{0,1},{1,0},{2,3},{3,2},{4,5},{5,4},{6,7},{7,6},{8,9},{9,8},{10,11... | collective-permute-start | bytes 786440 | tf_op jit(solution)/shard_map/ppermute | solution.py:340
  80.5 6.4 %collective-permute-start.11 = (bf16[8,128,256]{2,1,0:T(8,128)(2,1)S(1)}, bf16[8,128,256]{2,1,0:T(8,128)(2,1)S(1)}, u32[]{:S(2)}, u32[]{:S(2)}) collective-permute-start(bf16[8,128,256]{2,1,0:T(8,128)(2,1)S(1)} %collective-permute-done.3.mine1), channel_id=1, source_target_pairs={{0,1},{1,0},{2,3},{3,2},{4,5},{5,4},{6,7},{7,6},{8,9},{9,8},{10,11... | collective-permute-start | bytes 1572872 | tf_op jit(solution)/shard_map/ppermute | solution.py:351
  82.5 4.4 %collective-permute-start.12 = (bf16[8,128,256]{2,1,0:T(8,128)(2,1)S(1)}, bf16[8,128,256]{2,1,0:T(8,128)(2,1)S(1)}, u32[]{:S(2)}, u32[]{:S(2)}) collective-permute-start(bf16[8,128,256]{2,1,0:T(8,128)(2,1)S(1)} %collective-permute-done.4.mine3), channel_id=1, source_target_pairs={{0,1},{1,0},{2,3},{3,2},{4,5},{5,4},{6,7},{7,6},{8,9},{9,8},{10,11... | collective-permute-start | bytes 1572872 | tf_op jit(solution)/shard_map/ppermute | solution.py:351
  84.8 17.8 %collective-permute-start.10 = (bf16[8,128,256]{2,1,0:T(8,128)(2,1)S(1)}, bf16[8,128,256]{2,1,0:T(8,128)(2,1)S(1)}, u32[]{:S(2)}, u32[]{:S(2)}) collective-permute-start(bf16[8,128,256]{2,1,0:T(8,128)(2,1)S(1)} %collective-permute-done.5.mine), channel_id=1, source_target_pairs={{0,1},{1,0},{2,3},{3,2},{4,5},{5,4},{6,7},{7,6},{8,9},{9,8},{10,11... | collective-permute-start | bytes 1572872 | tf_op jit(solution)/shard_map/ppermute | solution.py:361
  106.2 23.0 %collective-permute-start.15 = (bf16[576,128]{1,0:T(8,128)(2,1)S(1)}, bf16[576,128]{1,0:T(8,128)(2,1)S(1)}, u32[]{:S(2)}, u32[]{:S(2)}) collective-permute-start(bf16[576,128]{1,0:T(8,128)(2,1)S(1)} %attend_last_3.1), channel_id=1, source_target_pairs={{0,4},{1,5},{2,6},{3,7},{4,8},{5,9},{6,10},{7,11},{8,12},{9,13},{1... | collective-permute-start | bytes 442376 | tf_op jit(solution)/shard_map/ppermute | solution.py:374
  111.9 17.3 %collective-permute-start.14 = (bf16[576,128]{1,0:T(8,128)(2,1)S(1)}, bf16[576,128]{1,0:T(8,128)(2,1)S(1)}, u32[]{:S(2)}, u32[]{:S(2)}) collective-permute-start(bf16[576,128]{1,0:T(8,128)(2,1)S(1)} %attend_last_2.1), channel_id=1, source_target_pairs={{0,8},{1,9},{2,10},{3,11},{4,12},{5,13},{6,14},{7,15},{8,0},{9,1},... | collective-permute-start | bytes 442376 | tf_op jit(solution)/shard_map/ppermute | solution.py:374
  120.2 14.3 %collective-permute-start.13 = (bf16[576,128]{1,0:T(8,128)(2,1)S(1)}, bf16[576,128]{1,0:T(8,128)(2,1)S(1)}, u32[]{:S(2)}, u32[]{:S(2)}) collective-permute-start(bf16[576,128]{1,0:T(8,128)(2,1)S(1)} %attend_last_1.1), channel_id=1, source_target_pairs={{0,12},{1,13},{2,14},{3,15},{4,0},{5,1},{6,2},{7,3},{8,4},{9,5},{1... | collective-permute-start | bytes 442376 | tf_op jit(solution)/shard_map/ppermute | solution.py:374
where the time goes:
time: 137 us; the launch traced here: 136 us
  starting transfers between devices  63.1 us (46%)
  Pallas kernels  49.8 us (36%)
  waiting for transfers between devices  20.1 us (15%)
  local copies, waits for them, and re-layouts  1.68 us (1%)
    pallas_call x1, Pallas kernels, on_device(): kernel_call(attend_next, 'attend_next', state_shape, [SMEM] * 2 + [VMEM]...  15.7 us
    all_to_all x1, starting transfers between devices, on_device(): arrived = lax.all_to_all(to_send, ('y', 'z'), 0, 0, tiled=True)  15.6 us
    ppermute x3, starting transfers between devices, on_device(): lax.ppermute(chunks[step], CHIPS, to_head_group(step))  14.4 us
    pallas_call x4, Pallas kernels, on_device(): kernel_call(functools.partial(attend_last, tile), f'attend_last_{tile}',...  14.4 us
    ppermute x3, starting transfers between devices, on_device(): lax.ppermute(mixed[step], CHIPS, to_head_group(-step))  12.1 us
    ppermute x3, waiting for transfers between devices, on_device(): lax.ppermute(chunks[step], CHIPS, to_head_group(step))  11.8 us
    pallas_call x1, Pallas kernels, on_device(): kernel_call(attend_own_x, 'attend_own_x', state_shape, [SMEM] * 2 + [VMEM...  10.6 us
    pallas_call x1, Pallas kernels, on_device(): kernel_call(attend_raw, 'attend_raw', state_shape, [SMEM] + [VMEM] * 11,...  5.95 us
  transfers between devices with their start and end apart: 17, of which 5 were waited for; matrix products, arithmetic and copies ran while one was open for 0% of the time, Pallas kernels for 32%

commit v1 on v0

--- a/solution.py
+++ b/solution.py
@@ -176,13 +176,13 @@
 HALVES = (slice(0, TILE // 2), slice(TILE // 2, TILE))
 
 
-def over_tiles(q_ref, m_ref, l_ref, a_ref, keys, values):
+def over_tiles(q_ref, first, m_ref, l_ref, a_ref, keys, values):
     def tile_step(tile, _):
         state = (m_ref.at[tile], l_ref.at[tile], a_ref.at[tile])
-        absorb_tile(q_ref.at[tile], state, keys, values)
+        absorb_tile(q_ref.at[first + tile], state, keys, values)
         return 0
 
-    lax.fori_loop(0, TILES, tile_step, 0)
+    lax.fori_loop(0, m_ref.shape[0], tile_step, 0)
 
 
 def attend_raw(
@@ -249,36 +249,23 @@
     l_ref[...] = jnp.zeros(l_ref.shape, F32)
     a_ref[...] = jnp.zeros(a_ref.shape, F32)
     count = list_visible(place, visible, (0,), chosen)
-    run = functools.partial(over_tiles, q_ref, m_ref, l_ref, a_ref)
+    run = functools.partial(over_tiles, q_ref, 0, m_ref, l_ref, a_ref)
     absorb_many(count, chosen, ((mine, other),), k_buf, v_buf, run)
 
 
-def attend_next(place, visible, q_ref, mine1, mine3, other1, other3, m_in, l_in, a_in, *rest):
-    m_ref, l_ref, a_ref, chosen, k_buf, v_buf = rest
-    m_ref[...] = m_in[...]
-    l_ref[...] = l_in[...]
-    a_ref[...] = a_in[...]
-    count = list_visible(place, visible, (1, 3), chosen)
-    absorb_many(
-        count,
-        chosen,
-        ((mine1, other1), (mine3, other3)),
-        k_buf,
-        v_buf,
-        functools.partial(over_tiles, q_ref, m_ref, l_ref, a_ref),
-    )
-
-
-def attend_last(tile, place, visible, q_ref, mine, other, m_in, l_in, a_in, out, *rest):
-    m_ref, l_ref, a_ref, chosen, k_buf, v_buf = rest
-    m_ref[...] = m_in[tile]
-    l_ref[...] = l_in[tile]
-    a_ref[...] = a_in[tile]
-    count = list_visible(place, visible, (2,), chosen)
-
-    run = functools.partial(absorb_tile, q_ref.at[tile], (m_ref, l_ref, a_ref))
-    absorb_many(count, chosen, ((mine, other),), k_buf, v_buf, run)
-    out[...] = (a_ref[...] / l_ref[...]).astype(BF16)
+def attend_prior(first, place, visible, q_ref, *rest):
+    sources = tuple(zip(rest[:3], rest[3:6]))
+    m_in, l_in, a_in, *outs = rest[6:-6]
+    m_ref, l_ref, a_ref, chosen, k_buf, v_buf = rest[-6:]
+    tiles = pl.ds(first, len(outs))
+    m_ref[...] = m_in[tiles]
+    l_ref[...] = l_in[tiles]
+    a_ref[...] = a_in[tiles]
+    count = list_visible(place, visible, (1, 3, 2), chosen)
+    run = functools.partial(over_tiles, q_ref, first, m_ref, l_ref, a_ref)
+    absorb_many(count, chosen, sources, k_buf, v_buf, run)
+    for tile, out in enumerate(outs):
+        out[...] = (a_ref[tile] / l_ref[tile]).astype(BF16)
 
 
 def unpack_outputs(place, r0, r1, r2, r3, tok_ref, bea_ref):
@@ -347,29 +334,21 @@
         byte_count=1000,
     )(place, bpos, asked, kv_o, kv_c, kv_z, kv_zc, block0, block0c, *state)
     arriving = [lax.ppermute(block0, CHIPS, to_later_x(step)) for step in (1, 3, 2)]
-    *near, far, _ = lax.optimization_barrier((*arriving, state[1]))
-    near_crossed = [lax.ppermute(block, CHIPS, OTHER_CORE) for block in near]
-    state = kernel_call(
-        attend_next,
-        "attend_next",
-        state_shape,
-        [SMEM] * 2 + [VMEM] * 8,
-        scratch,
-        flops=1000,
-        byte_count=1000,
-    )(place, visible, asked, *near, *near_crossed, *state)
-    far_crossed = lax.ppermute(far, CHIPS, OTHER_CORE)
-    mixed = [None] * TILES
-    for tile in (2, 1, 3, 0):
-        mixed[tile] = kernel_call(
-            functools.partial(attend_last, tile),
-            f"attend_last_{tile}",
-            jax.ShapeDtypeStruct((TILE, HD), BF16),
-            [SMEM] * 2 + [VMEM] * 6,
-            [pltpu.VMEM((TILE, HD), F32)] * 3 + scratch,
-            flops=1000,
-            byte_count=1000,
-        )(place, visible, asked, far, far_crossed, *state)
+    *arriving, _ = lax.optimization_barrier((*arriving, state[1]))
+    crossed = [lax.ppermute(block, CHIPS, OTHER_CORE) for block in arriving]
+    mixed = []
+    for first, tiles in ((1, 3), (0, 1)):
+        mixed = list(
+            kernel_call(
+                functools.partial(attend_prior, first),
+                f"attend_prior_{first}",
+                [jax.ShapeDtypeStruct((TILE, HD), BF16)] * tiles,
+                [SMEM] * 2 + [VMEM] * 10,
+                [pltpu.VMEM((tiles, TILE, HD), F32)] * 3 + scratch,
+                flops=1000,
+                byte_count=1000,
+            )(place, visible, asked, *arriving, *crossed, *state)
+        ) + mixed
     back = [mixed[0]] + [
         lax.ppermute(mixed[step], CHIPS, to_head_group(-step)) for step in range(1, TILES)
     ]

time: 137 us -> 129 us (0.942)
  the two profiles are of different devices: /device:TPU:63 before, /device:TPU:127 now
where the time goes in v1:
time: 129 us; the launch traced here: 128 us
  starting transfers between devices  65.3 us (51%)
  Pallas kernels  43.3 us (34%)
  waiting for transfers between devices  16.5 us (13%)
  local copies, waits for them, and re-layouts  1.68 us (1%)
    pallas_call x2, Pallas kernels, on_device(): kernel_call(functools.partial(attend_prior, first), f'attend_prior_{first...  27 us
    all_to_all x1, starting transfers between devices, on_device(): arrived = lax.all_to_all(to_send, ('y', 'z'), 0, 0, tiled=True)  14.7 us
    ppermute x3, starting transfers between devices, on_device(): lax.ppermute(chunks[step], CHIPS, to_head_group(step))  13.5 us
    ppermute x3, starting transfers between devices, on_device(): lax.ppermute(mixed[step], CHIPS, to_head_group(-step))  9.29 us
    ppermute x1, starting transfers between devices, on_device(): kv_z = lax.ppermute(kv_o, CHIPS, OTHER_PARITY)  8.88 us
    pallas_call x1, Pallas kernels, on_device(): kernel_call(attend_own_x, 'attend_own_x', state_shape, [SMEM] * 2 + [VMEM...  7.19 us
    ppermute x3, starting transfers between devices, on_device(): crossed = [lax.ppermute(block, CHIPS, OTHER_CORE) for block in arriving]  6.37 us
    ppermute x3, waiting for transfers between devices, on_device(): lax.ppermute(chunks[step], CHIPS, to_head_group(step))  6.03 us
  transfers between devices with their start and end apart: 17, of which 7 were waited for; matrix products, arithmetic and copies ran while one was open for 0% of the time, Pallas kernels for 17%

profile of v1, /device:TPU:127, one launch (start us, length us, event | category | flops | bytes accessed | tf_op | source)
XLA Modules:
  0.0 128.0 jit_solution(9220194608099538079)
XLA Ops:
  0.7 0.8 copy-done.5
  1.5 0.7 copy-done.6
  2.2 0.8 pack_beacons.1
  3.0 14.7 %all-to-all-start = ((bf16[64,16,256]{2,1,0:T(8,128)(2,1)}), bf16[64,16,256]{2,1,0:T(8,128)(2,1)S(1)}, u32[]{:S(2)}, u32[]{:S(2)}) async-start(bf16[64,16,256]{2,1,0:T(8,128)(2,1)} %pack_beacons.1), calls=%async_computation | async-start | bytes 1048576 | tf_op jit(solution)/shard_map/all_to_all | solution.py:301
  17.8 0.8 pack_tokens.1
  18.6 4.0 %collective-permute-start = (bf16[832,128]{1,0:T(8,128)(2,1)S(1)}, bf16[832,128]{1,0:T(8,128)(2,1)S(1)}, u32[]{:S(2)}, u32[]{:S(2)}) collective-permute-start(bf16[832,128]{1,0:T(8,128)(2,1)S(1)} %get-tuple-element.24), channel_id=1, source_target_pairs={{0,4},{1,5},{2,6},{3,7},{4,8},{5,9},{6,10},{7,11},{8,12},{9,13},{1... | collective-permute-start | bytes 638984 | tf_op jit(solution)/shard_map/ppermute | solution.py:292
  22.6 4.3 %collective-permute-start.1 = (bf16[832,128]{1,0:T(8,128)(2,1)S(1)}, bf16[832,128]{1,0:T(8,128)(2,1)S(1)}, u32[]{:S(2)}, u32[]{:S(2)}) collective-permute-start(bf16[832,128]{1,0:T(8,128)(2,1)S(1)} %get-tuple-element.25), channel_id=1, source_target_pairs={{0,8},{1,9},{2,10},{3,11},{4,12},{5,13},{6,14},{7,15},{8,0},{9,1},... | collective-permute-start | bytes 638984 | tf_op jit(solution)/shard_map/ppermute | solution.py:292
  26.9 5.2 %collective-permute-start.2 = (bf16[832,128]{1,0:T(8,128)(2,1)S(1)}, bf16[832,128]{1,0:T(8,128)(2,1)S(1)}, u32[]{:S(2)}, u32[]{:S(2)}) collective-permute-start(bf16[832,128]{1,0:T(8,128)(2,1)S(1)} %get-tuple-element.26), channel_id=1, source_target_pairs={{0,12},{1,13},{2,14},{3,15},{4,0},{5,1},{6,2},{7,3},{8,4},{9,5},{1... | collective-permute-start | bytes 638984 | tf_op jit(solution)/shard_map/ppermute | solution.py:292
  32.1 1.9 %all-to-all-done = bf16[64,16,256]{2,1,0:T(8,128)(2,1)S(1)} async-done(((bf16[64,16,256]{2,1,0:T(8,128)(2,1)}), bf16[64,16,256]{2,1,0:T(8,128)(2,1)S(1)}, u32[]{:S(2)}, u32[]{:S(2)}) %all-to-all-start) | async-done | bytes 524320 | tf_op jit(solution)/shard_map/all_to_all | solution.py:301
  34.0 3.8 %collective-permute-start.8 = (bf16[8,128,256]{2,1,0:T(8,128)(2,1)S(1)}, bf16[8,128,256]{2,1,0:T(8,128)(2,1)S(1)}, u32[]{:S(2)}, u32[]{:S(2)}) collective-permute-start(bf16[8,128,256]{2,1,0:T(8,128)(2,1)S(1)} %bitcast.21), channel_id=1, source_target_pairs={{0,1},{1,0},{2,3},{3,2},{4,5},{5,4},{6,7},{7,6},{8,9},{9,8},{10,11... | collective-permute-start | bytes 1572872 | tf_op jit(solution)/shard_map/ppermute | solution.py:307
  37.9 1.3 %collective-permute-start.3 = (bf16[8,128,256]{2,1,0:T(8,128)(2,1)S(1)}, bf16[8,128,256]{2,1,0:T(8,128)(2,1)S(1)}, u32[]{:S(2)}, u32[]{:S(2)}) collective-permute-start(bf16[8,128,256]{2,1,0:T(8,128)(2,1)S(1)} %bitcast.22), channel_id=1, source_target_pairs={{0,128},{1,129},{2,130},{3,131},{4,132},{5,133},{6,134},{7,135},{8... | collective-permute-start | bytes 1572872 | tf_op jit(solution)/shard_map/ppermute | solution.py:336
  39.2 5.4 %collective-permute-done = bf16[832,128]{1,0:T(8,128)(2,1)S(1)} collective-permute-done((bf16[832,128]{1,0:T(8,128)(2,1)S(1)}, bf16[832,128]{1,0:T(8,128)(2,1)S(1)}, u32[]{:S(2)}, u32[]{:S(2)}) %collective-permute-start) | collective-permute-done | bytes 213024 | tf_op jit(solution)/shard_map/ppermute | solution.py:292
  44.6 1.3 %collective-permute-start.4 = (bf16[8,128,256]{2,1,0:T(8,128)(2,1)S(1)}, bf16[8,128,256]{2,1,0:T(8,128)(2,1)S(1)}, u32[]{:S(2)}, u32[]{:S(2)}) collective-permute-start(bf16[8,128,256]{2,1,0:T(8,128)(2,1)S(1)} %bitcast.23), channel_id=1, source_target_pairs={{0,384},{1,385},{2,386},{3,387},{4,388},{5,389},{6,390},{7,391},{8... | collective-permute-start | bytes 1572872 | tf_op jit(solution)/shard_map/ppermute | solution.py:336
  45.9 1.3 %collective-permute-start.5 = (bf16[8,128,256]{2,1,0:T(8,128)(2,1)S(1)}, bf16[8,128,256]{2,1,0:T(8,128)(2,1)S(1)}, u32[]{:S(2)}, u32[]{:S(2)}) collective-permute-start(bf16[8,128,256]{2,1,0:T(8,128)(2,1)S(1)} %bitcast.24), channel_id=1, source_target_pairs={{0,256},{1,257},{2,258},{3,259},{4,260},{5,261},{6,262},{7,263},{8... | collective-permute-start | bytes 1572872 | tf_op jit(solution)/shard_map/ppermute | solution.py:336
  47.9 8.9 %collective-permute-start.7 = (bf16[4,256,128]{2,1,0:T(8,128)(2,1)S(1)}, bf16[4,256,128]{2,1,0:T(8,128)(2,1)S(1)}, u32[]{:S(2)}, u32[]{:S(2)}) collective-permute-start(bf16[4,256,128]{2,1,0:T(8,128)(2,1)S(1)} %pad_maximum_fusion.1.kv_o), channel_id=1, source_target_pairs={{0,2},{1,3},{2,0},{3,1},{4,6},{5,7},{6,4},{7,5},{8,10},{9,11},{10,... | collective-permute-start | bytes 786440 | tf_op jit(solution)/shard_map/ppermute | solution.py:324
  56.9 3.0 %collective-permute-start.6 = (bf16[4,256,128]{2,1,0:T(8,128)(2,1)S(1)}, bf16[4,256,128]{2,1,0:T(8,128)(2,1)S(1)}, u32[]{:S(2)}, u32[]{:S(2)}) collective-permute-start(bf16[4,256,128]{2,1,0:T(8,128)(2,1)S(1)} %pad_maximum_fusion.1.kv_o), channel_id=1, source_target_pairs={{0,1},{1,0},{2,3},{3,2},{4,5},{5,4},{6,7},{7,6},{8,9},{9,8},{10,11... | collective-permute-start | bytes 786440 | tf_op jit(solution)/shard_map/ppermute | solution.py:325
  59.9 7.2 %attend_own_x.1 = (f32[4,576,128]{2,1,0:T(8,128)S(1)}, f32[4,576,128]{2,1,0:T(8,128)S(1)}, f32[4,576,128]{2,1,0:T(8,128)S(1)}) custom-call(s32[4]{0:T(128)S(1)} %pad_add_fusion.place, s32[32,32]{1,0:T(8,128)S(1)} %copy-done.1, bf16[4,576,128]{2,1,0:T(8,128)(2,1)S(1)} %pad_maximum_fusion.q_ref, bf16[8,128,256]{2,1,0:T(8,128)(2,1)S(1)} %bitcast.25, ...), custom_call_target="tpu_custom_call" | custom-call | flops 1000 | bytes 1000 | tf_op jit(solution)/shard_map/attend_own_x/pallas_call | solution.py:315
  67.1 1.9 %collective-permute-start.9 = (bf16[4,256,128]{2,1,0:T(8,128)(2,1)S(1)}, bf16[4,256,128]{2,1,0:T(8,128)(2,1)S(1)}, u32[]{:S(2)}, u32[]{:S(2)}) collective-permute-start(bf16[4,256,128]{2,1,0:T(8,128)(2,1)S(1)} %collective-permute-done.7.kv_z), channel_id=1, source_target_pairs={{0,1},{1,0},{2,3},{3,2},{4,5},{5,4},{6,7},{7,6},{8,9},{9,8},{10,11... | collective-permute-start | bytes 786440 | tf_op jit(solution)/shard_map/ppermute | solution.py:327
  69.1 1.5 %collective-permute-done.9.kv_zc = bf16[4,256,128]{2,1,0:T(8,128)(2,1)S(1)} collective-permute-done((bf16[4,256,128]{2,1,0:T(8,128)(2,1)S(1)}, bf16[4,256,128]{2,1,0:T(8,128)(2,1)S(1)}, u32[]{:S(2)}, u32[]{:S(2)}) %collective-permute-start.9) | collective-permute-done | bytes 262176 | tf_op jit(solution)/shard_map/ppermute | solution.py:327
  70.6 5.9 %attend_raw.1 = (f32[4,576,128]{2,1,0:T(8,128)S(1)}, f32[4,576,128]{2,1,0:T(8,128)S(1)}, f32[4,576,128]{2,1,0:T(8,128)S(1)}) custom-call(s32[4]{0:T(128)S(1)} %pad_add_fusion.place, s32[256,128]{1,0:T(8,128)S(1)} %broadcast_in_dim.2.bpos, bf16[4,576,128]{2,1,0:T(8,128)(2,1)S(1)} %pad_maximum_fusion.q_ref, bf16[4,256,128]{2,1,0:T(8,128)(2,1)S(1)} %pad_maximum_fusion.1.kv_o, ...), custom_call_target="tpu_custom_call" | custom-call | flops 1000 | bytes 1000 | tf_op jit(solution)/shard_map/attend_raw/pallas_call | solution.py:328
  76.6 2.0 %collective-permute-start.10 = (bf16[8,128,256]{2,1,0:T(8,128)(2,1)S(1)}, bf16[8,128,256]{2,1,0:T(8,128)(2,1)S(1)}, u32[]{:S(2)}, u32[]{:S(2)}) collective-permute-start(bf16[8,128,256]{2,1,0:T(8,128)(2,1)S(1)} %collective-permute-done.3.rest_0_), channel_id=1, source_target_pairs={{0,1},{1,0},{2,3},{3,2},{4,5},{5,4},{6,7},{7,6},{8,9},{9,8},{10,11... | collective-permute-start | bytes 1572872 | tf_op jit(solution)/shard_map/ppermute | solution.py:338
  78.7 2.3 %collective-permute-start.11 = (bf16[8,128,256]{2,1,0:T(8,128)(2,1)S(1)}, bf16[8,128,256]{2,1,0:T(8,128)(2,1)S(1)}, u32[]{:S(2)}, u32[]{:S(2)}) collective-permute-start(bf16[8,128,256]{2,1,0:T(8,128)(2,1)S(1)} %collective-permute-done.4.rest_1_), channel_id=1, source_target_pairs={{0,1},{1,0},{2,3},{3,2},{4,5},{5,4},{6,7},{7,6},{8,9},{9,8},{10,11... | collective-permute-start | bytes 1572872 | tf_op jit(solution)/shard_map/ppermute | solution.py:338
  81.0 2.0 %collective-permute-start.12 = (bf16[8,128,256]{2,1,0:T(8,128)(2,1)S(1)}, bf16[8,128,256]{2,1,0:T(8,128)(2,1)S(1)}, u32[]{:S(2)}, u32[]{:S(2)}) collective-permute-start(bf16[8,128,256]{2,1,0:T(8,128)(2,1)S(1)} %collective-permute-done.5.rest_2_), channel_id=1, source_target_pairs={{0,1},{1,0},{2,3},{3,2},{4,5},{5,4},{6,7},{7,6},{8,9},{9,8},{10,11... | collective-permute-start | bytes 1572872 | tf_op jit(solution)/shard_map/ppermute | solution.py:338
  83.0 1.7 %collective-permute-done.12.rest_5_ = bf16[8,128,256]{2,1,0:T(8,128)(2,1)S(1)} collective-permute-done((bf16[8,128,256]{2,1,0:T(8,128)(2,1)S(1)}, bf16[8,128,256]{2,1,0:T(8,128)(2,1)S(1)}, u32[]{:S(2)}, u32[]{:S(2)}) %collective-permute-start.12) | collective-permute-done | bytes 524320 | tf_op jit(solution)/shard_map/ppermute | solution.py:338
  84.8 19.2 %attend_prior_1.1 = (bf16[576,128]{1,0:T(8,128)(2,1)S(1)}, bf16[576,128]{1,0:T(8,128)(2,1)S(1)}, bf16[576,128]{1,0:T(8,128)(2,1)S(1)}) custom-call(s32[4]{0:T(128)S(1)} %pad_add_fusion.place, s32[32,32]{1,0:T(8,128)S(1)} %copy-done.1, bf16[4,576,128]{2,1,0:T(8,128)(2,1)S(1)} %pad_maximum_fusion.q_ref, ...), custom_call_target="tpu_custom_call" | custom-call | flops 1000 | bytes 1000 | tf_op jit(solution)/shard_map/attend_prior_1/pallas_call | solution.py:342
  104.0 2.0 %collective-permute-start.13 = (bf16[576,128]{1,0:T(8,128)(2,1)S(1)}, bf16[576,128]{1,0:T(8,128)(2,1)S(1)}, u32[]{:S(2)}, u32[]{:S(2)}) collective-permute-start(bf16[576,128]{1,0:T(8,128)(2,1)S(1)} %get-tuple-element.41), channel_id=1, source_target_pairs={{0,12},{1,13},{2,14},{3,15},{4,0},{5,1},{6,2},{7,3},{8,4},{9,5},{1... | collective-permute-start | bytes 442376 | tf_op jit(solution)/shard_map/ppermute | solution.py:353
  106.0 5.4 %collective-permute-start.14 = (bf16[576,128]{1,0:T(8,128)(2,1)S(1)}, bf16[576,128]{1,0:T(8,128)(2,1)S(1)}, u32[]{:S(2)}, u32[]{:S(2)}) collective-permute-start(bf16[576,128]{1,0:T(8,128)(2,1)S(1)} %get-tuple-element.42), channel_id=1, source_target_pairs={{0,8},{1,9},{2,10},{3,11},{4,12},{5,13},{6,14},{7,15},{8,0},{9,1},... | collective-permute-start | bytes 442376 | tf_op jit(solution)/shard_map/ppermute | solution.py:353
  111.4 1.9 %collective-permute-start.15 = (bf16[576,128]{1,0:T(8,128)(2,1)S(1)}, bf16[576,128]{1,0:T(8,128)(2,1)S(1)}, u32[]{:S(2)}, u32[]{:S(2)}) collective-permute-start(bf16[576,128]{1,0:T(8,128)(2,1)S(1)} %get-tuple-element.43), channel_id=1, source_target_pairs={{0,4},{1,5},{2,6},{3,7},{4,8},{5,9},{6,10},{7,11},{8,12},{9,13},{1... | collective-permute-start | bytes 442376 | tf_op jit(solution)/shard_map/ppermute | solution.py:353
  113.3 7.8 %attend_prior_0.1.r0 = bf16[576,128]{1,0:T(8,128)(2,1)S(1)} custom-call(s32[4]{0:T(128)S(1)} %pad_add_fusion.place, s32[32,32]{1,0:T(8,128)S(1)} %copy-done.1, bf16[4,576,128]{2,1,0:T(8,128)(2,1)S(1)} %pad_maximum_fusion.q_ref, bf16[8,128,256]{2,1,0:T(8,128)(2,1)S(1)} %collective-permute-done.3.rest_0_, ...), custom_call_target="tpu_custom_call" | custom-call | flops 1000 | bytes 1000 | tf_op jit(solution)/shard_map/attend_prior_0/pallas_call | solution.py:342
  121.2 1.9 %collective-permute-done.14.r2 = bf16[576,128]{1,0:T(8,128)(2,1)S(1)} collective-permute-done((bf16[576,128]{1,0:T(8,128)(2,1)S(1)}, bf16[576,128]{1,0:T(8,128)(2,1)S(1)}, u32[]{:S(2)}, u32[]{:S(2)}) %collective-permute-start.14) | collective-permute-done | bytes 147488 | tf_op jit(solution)/shard_map/ppermute | solution.py:353
  123.1 3.4 %collective-permute-done.15.r3 = bf16[576,128]{1,0:T(8,128)(2,1)S(1)} collective-permute-done((bf16[576,128]{1,0:T(8,128)(2,1)S(1)}, bf16[576,128]{1,0:T(8,128)(2,1)S(1)}, u32[]{:S(2)}, u32[]{:S(2)}) %collective-permute-start.15) | collective-permute-done | bytes 147488 | tf_op jit(solution)/shard_map/ppermute | solution.py:353
  126.5 1.5 %unpack_outputs.1 = (bf16[128,2048]{1,0:T(8,128)(2,1)}, bf16[16,2048]{1,0:T(8,128)(2,1)}) custom-call(s32[4]{0:T(128)S(1)} %pad_add_fusion.place, bf16[576,128]{1,0:T(8,128)(2,1)S(1)} %attend_prior_0.1.r0, bf16[576,128]{1,0:T(8,128)(2,1)S(1)} %collective-permute-done.13.r1, bf16[576,128]{1,0:T(8,128)(2,1)S(1)} %collective-permute-done.14.r2, ...), custom_call_target="tpu_custom_call" | custom-call | bytes 1000 | tf_op jit(solution)/shard_map/unpack_outputs/pallas_call | solution.py:355
  (33 shorter events, 1.0 us)
Async XLA Ops:
  0.6 17.2 %copy-start.3 = (bf16[128,512]{1,0:T(8,128)(2,1)S(1)}, bf16[128,512]{1,0:T(8,128)(2,1)}, u32[]{:S(2)}) copy-start(bf16[128,512]{1,0:T(8,128)(2,1)} %v_ref.2) | copy-start | bytes 393220
  0.6 17.2 %copy-start.4 = (bf16[16,2048]{1,0:T(8,128)(2,1)S(1)}, bf16[16,2048]{1,0:T(8,128)(2,1)}, u32[]{:S(2)}) copy-start(bf16[16,2048]{1,0:T(8,128)(2,1)} %bq_ref.1) | copy-start | bytes 196612
  0.7 17.2 %copy-start = (bf16[128,2048]{1,0:T(8,128)(2,1)S(1)}, bf16[128,2048]{1,0:T(8,128)(2,1)}, u32[]{:S(2)}) copy-start(bf16[128,2048]{1,0:T(8,128)(2,1)} %q_ref.1) | copy-start | bytes 1572868
  0.7 17.2 %copy-start.2 = (bf16[128,512]{1,0:T(8,128)(2,1)S(1)}, bf16[128,512]{1,0:T(8,128)(2,1)}, u32[]{:S(2)}) copy-start(bf16[128,512]{1,0:T(8,128)(2,1)} %k_ref.2) | copy-start | bytes 393220
  0.7 0.8 copy-start.5
  1.5 0.7 copy-start.6
  3.0 31.0 %all-to-all-start = ((bf16[64,16,256]{2,1,0:T(8,128)(2,1)}), bf16[64,16,256]{2,1,0:T(8,128)(2,1)S(1)}, u32[]{:S(2)}, u32[]{:S(2)}) async-start(bf16[64,16,256]{2,1,0:T(8,128)(2,1)} %pack_beacons.1), calls=%async_computation | async-start | bytes 1048576 | tf_op jit(solution)/shard_map/all_to_all | solution.py:301
  18.6 26.0 %collective-permute-start = (bf16[832,128]{1,0:T(8,128)(2,1)S(1)}, bf16[832,128]{1,0:T(8,128)(2,1)S(1)}, u32[]{:S(2)}, u32[]{:S(2)}) collective-permute-start(bf16[832,128]{1,0:T(8,128)(2,1)S(1)} %get-tuple-element.24), channel_id=1, source_target_pairs={{0,4},{1,5},{2,6},{3,7},{4,8},{5,9},{6,10},{7,11},{8,12},{9,13},{1... | collective-permute-start | bytes 638984 | tf_op jit(solution)/shard_map/ppermute | solution.py:292
  22.6 23.3 %collective-permute-start.1 = (bf16[832,128]{1,0:T(8,128)(2,1)S(1)}, bf16[832,128]{1,0:T(8,128)(2,1)S(1)}, u32[]{:S(2)}, u32[]{:S(2)}) collective-permute-start(bf16[832,128]{1,0:T(8,128)(2,1)S(1)} %get-tuple-element.25), channel_id=1, source_target_pairs={{0,8},{1,9},{2,10},{3,11},{4,12},{5,13},{6,14},{7,15},{8,0},{9,1},... | collective-permute-start | bytes 638984 | tf_op jit(solution)/shard_map/ppermute | solution.py:292
  26.9 20.9 %collective-permute-start.2 = (bf16[832,128]{1,0:T(8,128)(2,1)S(1)}, bf16[832,128]{1,0:T(8,128)(2,1)S(1)}, u32[]{:S(2)}, u32[]{:S(2)}) collective-permute-start(bf16[832,128]{1,0:T(8,128)(2,1)S(1)} %get-tuple-element.26), channel_id=1, source_target_pairs={{0,12},{1,13},{2,14},{3,15},{4,0},{5,1},{6,2},{7,3},{8,4},{9,5},{1... | collective-permute-start | bytes 638984 | tf_op jit(solution)/shard_map/ppermute | solution.py:292
  34.0 22.9 %collective-permute-start.8 = (bf16[8,128,256]{2,1,0:T(8,128)(2,1)S(1)}, bf16[8,128,256]{2,1,0:T(8,128)(2,1)S(1)}, u32[]{:S(2)}, u32[]{:S(2)}) collective-permute-start(bf16[8,128,256]{2,1,0:T(8,128)(2,1)S(1)} %bitcast.21), channel_id=1, source_target_pairs={{0,1},{1,0},{2,3},{3,2},{4,5},{5,4},{6,7},{7,6},{8,9},{9,8},{10,11... | collective-permute-start | bytes 1572872 | tf_op jit(solution)/shard_map/ppermute | solution.py:307
  37.9 38.7 %collective-permute-start.3 = (bf16[8,128,256]{2,1,0:T(8,128)(2,1)S(1)}, bf16[8,128,256]{2,1,0:T(8,128)(2,1)S(1)}, u32[]{:S(2)}, u32[]{:S(2)}) collective-permute-start(bf16[8,128,256]{2,1,0:T(8,128)(2,1)S(1)} %bitcast.22), channel_id=1, source_target_pairs={{0,128},{1,129},{2,130},{3,131},{4,132},{5,133},{6,134},{7,135},{8... | collective-permute-start | bytes 1572872 | tf_op jit(solution)/shard_map/ppermute | solution.py:336
  44.6 32.0 %collective-permute-start.4 = (bf16[8,128,256]{2,1,0:T(8,128)(2,1)S(1)}, bf16[8,128,256]{2,1,0:T(8,128)(2,1)S(1)}, u32[]{:S(2)}, u32[]{:S(2)}) collective-permute-start(bf16[8,128,256]{2,1,0:T(8,128)(2,1)S(1)} %bitcast.23), channel_id=1, source_target_pairs={{0,384},{1,385},{2,386},{3,387},{4,388},{5,389},{6,390},{7,391},{8... | collective-permute-start | bytes 1572872 | tf_op jit(solution)/shard_map/ppermute | solution.py:336
  45.9 30.7 %collective-permute-start.5 = (bf16[8,128,256]{2,1,0:T(8,128)(2,1)S(1)}, bf16[8,128,256]{2,1,0:T(8,128)(2,1)S(1)}, u32[]{:S(2)}, u32[]{:S(2)}) collective-permute-start(bf16[8,128,256]{2,1,0:T(8,128)(2,1)S(1)} %bitcast.24), channel_id=1, source_target_pairs={{0,256},{1,257},{2,258},{3,259},{4,260},{5,261},{6,262},{7,263},{8... | collective-permute-start | bytes 1572872 | tf_op jit(solution)/shard_map/ppermute | solution.py:336
  47.9 12.0 %copy-start.1 = (s32[32,32]{1,0:T(8,128)S(1)}, s32[32,32]{1,0:T(8,128)}, u32[]{:S(2)}) copy-start(s32[32,32]{1,0:T(8,128)} %visible.5) | copy-start | bytes 12292
  47.9 19.2 %collective-permute-start.7 = (bf16[4,256,128]{2,1,0:T(8,128)(2,1)S(1)}, bf16[4,256,128]{2,1,0:T(8,128)(2,1)S(1)}, u32[]{:S(2)}, u32[]{:S(2)}) collective-permute-start(bf16[4,256,128]{2,1,0:T(8,128)(2,1)S(1)} %pad_maximum_fusion.1.kv_o), channel_id=1, source_target_pairs={{0,2},{1,3},{2,0},{3,1},{4,6},{5,7},{6,4},{7,5},{8,10},{9,11},{10,... | collective-permute-start | bytes 786440 | tf_op jit(solution)/shard_map/ppermute | solution.py:324
  56.8 13.7 %copy-start.7 = (s32[256]{0:T(256)S(1)}, s32[256]{0:T(256)}, u32[]{:S(2)}) copy-start(s32[256]{0:T(256)} %param.14) | copy-start | bytes 3076
  56.9 12.1 %collective-permute-start.6 = (bf16[4,256,128]{2,1,0:T(8,128)(2,1)S(1)}, bf16[4,256,128]{2,1,0:T(8,128)(2,1)S(1)}, u32[]{:S(2)}, u32[]{:S(2)}) collective-permute-start(bf16[4,256,128]{2,1,0:T(8,128)(2,1)S(1)} %pad_maximum_fusion.1.kv_o), channel_id=1, source_target_pairs={{0,1},{1,0},{2,3},{3,2},{4,5},{5,4},{6,7},{7,6},{8,9},{9,8},{10,11... | collective-permute-start | bytes 786440 | tf_op jit(solution)/shard_map/ppermute | solution.py:325
  67.1 3.4 %collective-permute-start.9 = (bf16[4,256,128]{2,1,0:T(8,128)(2,1)S(1)}, bf16[4,256,128]{2,1,0:T(8,128)(2,1)S(1)}, u32[]{:S(2)}, u32[]{:S(2)}) collective-permute-start(bf16[4,256,128]{2,1,0:T(8,128)(2,1)S(1)} %collective-permute-done.7.kv_z), channel_id=1, source_target_pairs={{0,1},{1,0},{2,3},{3,2},{4,5},{5,4},{6,7},{7,6},{8,9},{9,8},{10,11... | collective-permute-start | bytes 786440 | tf_op jit(solution)/shard_map/ppermute | solution.py:327
  76.6 6.4 %collective-permute-start.10 = (bf16[8,128,256]{2,1,0:T(8,128)(2,1)S(1)}, bf16[8,128,256]{2,1,0:T(8,128)(2,1)S(1)}, u32[]{:S(2)}, u32[]{:S(2)}) collective-permute-start(bf16[8,128,256]{2,1,0:T(8,128)(2,1)S(1)} %collective-permute-done.3.rest_0_), channel_id=1, source_target_pairs={{0,1},{1,0},{2,3},{3,2},{4,5},{5,4},{6,7},{7,6},{8,9},{9,8},{10,11... | collective-permute-start | bytes 1572872 | tf_op jit(solution)/shard_map/ppermute | solution.py:338
  78.7 4.4 %collective-permute-start.11 = (bf16[8,128,256]{2,1,0:T(8,128)(2,1)S(1)}, bf16[8,128,256]{2,1,0:T(8,128)(2,1)S(1)}, u32[]{:S(2)}, u32[]{:S(2)}) collective-permute-start(bf16[8,128,256]{2,1,0:T(8,128)(2,1)S(1)} %collective-permute-done.4.rest_1_), channel_id=1, source_target_pairs={{0,1},{1,0},{2,3},{3,2},{4,5},{5,4},{6,7},{7,6},{8,9},{9,8},{10,11... | collective-permute-start | bytes 1572872 | tf_op jit(solution)/shard_map/ppermute | solution.py:338
  81.0 3.8 %collective-permute-start.12 = (bf16[8,128,256]{2,1,0:T(8,128)(2,1)S(1)}, bf16[8,128,256]{2,1,0:T(8,128)(2,1)S(1)}, u32[]{:S(2)}, u32[]{:S(2)}) collective-permute-start(bf16[8,128,256]{2,1,0:T(8,128)(2,1)S(1)} %collective-permute-done.5.rest_2_), channel_id=1, source_target_pairs={{0,1},{1,0},{2,3},{3,2},{4,5},{5,4},{6,7},{7,6},{8,9},{9,8},{10,11... | collective-permute-start | bytes 1572872 | tf_op jit(solution)/shard_map/ppermute | solution.py:338
  104.0 17.1 %collective-permute-start.13 = (bf16[576,128]{1,0:T(8,128)(2,1)S(1)}, bf16[576,128]{1,0:T(8,128)(2,1)S(1)}, u32[]{:S(2)}, u32[]{:S(2)}) collective-permute-start(bf16[576,128]{1,0:T(8,128)(2,1)S(1)} %get-tuple-element.41), channel_id=1, source_target_pairs={{0,12},{1,13},{2,14},{3,15},{4,0},{5,1},{6,2},{7,3},{8,4},{9,5},{1... | collective-permute-start | bytes 442376 | tf_op jit(solution)/shard_map/ppermute | solution.py:353
  106.0 17.1 %collective-permute-start.14 = (bf16[576,128]{1,0:T(8,128)(2,1)S(1)}, bf16[576,128]{1,0:T(8,128)(2,1)S(1)}, u32[]{:S(2)}, u32[]{:S(2)}) collective-permute-start(bf16[576,128]{1,0:T(8,128)(2,1)S(1)} %get-tuple-element.42), channel_id=1, source_target_pairs={{0,8},{1,9},{2,10},{3,11},{4,12},{5,13},{6,14},{7,15},{8,0},{9,1},... | collective-permute-start | bytes 442376 | tf_op jit(solution)/shard_map/ppermute | solution.py:353
  111.4 15.1 %collective-permute-start.15 = (bf16[576,128]{1,0:T(8,128)(2,1)S(1)}, bf16[576,128]{1,0:T(8,128)(2,1)S(1)}, u32[]{:S(2)}, u32[]{:S(2)}) collective-permute-start(bf16[576,128]{1,0:T(8,128)(2,1)S(1)} %get-tuple-element.43), channel_id=1, source_target_pairs={{0,4},{1,5},{2,6},{3,7},{4,8},{5,9},{6,10},{7,11},{8,12},{9,13},{1... | collective-permute-start | bytes 442376 | tf_op jit(solution)/shard_map/ppermute | solution.py:353

commit v2 on v1

--- a/solution.py
+++ b/solution.py
@@ -337,7 +337,7 @@
     *arriving, _ = lax.optimization_barrier((*arriving, state[1]))
     crossed = [lax.ppermute(block, CHIPS, OTHER_CORE) for block in arriving]
     mixed = []
-    for first, tiles in ((1, 3), (0, 1)):
+    for first, tiles in ((2, 2), (1, 1), (0, 1)):
         mixed = list(
             kernel_call(
                 functools.partial(attend_prior, first),

time: 129 us -> 129 us (level)
  the two profiles are of different devices: /device:TPU:127 before, /device:TPU:14 now
where the time goes in v2:
time: 129 us; the launch traced here: 128 us
  starting transfers between devices  64.1 us (50%)
  Pallas kernels  44 us (34%)
  waiting for transfers between devices  16.8 us (13%)
  local copies, waits for them, and re-layouts  1.68 us (1%)
    pallas_call x3, Pallas kernels, on_device(): kernel_call(functools.partial(attend_prior, first), f'attend_prior_{first...  29.2 us
    all_to_all x1, starting transfers between devices, on_device(): arrived = lax.all_to_all(to_send, ('y', 'z'), 0, 0, tiled=True)  16.6 us
    ppermute x3, starting transfers between devices, on_device(): lax.ppermute(chunks[step], CHIPS, to_head_group(step))  15.2 us
    ppermute x3, starting transfers between devices, on_device(): lax.ppermute(mixed[step], CHIPS, to_head_group(-step))  13.8 us
    ppermute x3, waiting for transfers between devices, on_device(): lax.ppermute(chunks[step], CHIPS, to_head_group(step))  11.5 us
    ppermute x3, starting transfers between devices, on_device(): crossed = [lax.ppermute(block, CHIPS, OTHER_CORE) for block in arriving]  6.61 us
    pallas_call x1, Pallas kernels, on_device(): kernel_call(attend_raw, 'attend_raw', state_shape, [SMEM] + [VMEM] * 11,...  5.94 us
    pallas_call x1, Pallas kernels, on_device(): kernel_call(attend_own_x, 'attend_own_x', state_shape, [SMEM] * 2 + [VMEM...  5.8 us
  transfers between devices with their start and end apart: 17, of which 6 were waited for; matrix products, arithmetic and copies ran while one was open for 0% of the time, Pallas kernels for 22%

profile of v2, /device:TPU:14, one launch (start us, length us, event | category | flops | bytes accessed | tf_op | source)
XLA Modules:
  0.0 127.8 jit_solution(15697070903497963402)
XLA Ops:
  0.7 0.8 copy-done.5
  1.5 0.7 copy-done.6
  2.2 0.8 pack_beacons.1
  3.0 16.6 %all-to-all-start = ((bf16[64,16,256]{2,1,0:T(8,128)(2,1)}), bf16[64,16,256]{2,1,0:T(8,128)(2,1)S(1)}, u32[]{:S(2)}, u32[]{:S(2)}) async-start(bf16[64,16,256]{2,1,0:T(8,128)(2,1)} %pack_beacons.1), calls=%async_computation | async-start | bytes 1048576 | tf_op jit(solution)/shard_map/all_to_all | solution.py:301
  19.7 0.8 pack_tokens.1
  20.5 4.3 %collective-permute-start = (bf16[832,128]{1,0:T(8,128)(2,1)S(1)}, bf16[832,128]{1,0:T(8,128)(2,1)S(1)}, u32[]{:S(2)}, u32[]{:S(2)}) collective-permute-start(bf16[832,128]{1,0:T(8,128)(2,1)S(1)} %get-tuple-element.23), channel_id=1, source_target_pairs={{0,4},{1,5},{2,6},{3,7},{4,8},{5,9},{6,10},{7,11},{8,12},{9,13},{1... | collective-permute-start | bytes 638984 | tf_op jit(solution)/shard_map/ppermute | solution.py:292
  24.7 5.5 %collective-permute-start.1 = (bf16[832,128]{1,0:T(8,128)(2,1)S(1)}, bf16[832,128]{1,0:T(8,128)(2,1)S(1)}, u32[]{:S(2)}, u32[]{:S(2)}) collective-permute-start(bf16[832,128]{1,0:T(8,128)(2,1)S(1)} %get-tuple-element.24), channel_id=1, source_target_pairs={{0,8},{1,9},{2,10},{3,11},{4,12},{5,13},{6,14},{7,15},{8,0},{9,1},... | collective-permute-start | bytes 638984 | tf_op jit(solution)/shard_map/ppermute | solution.py:292
  30.2 5.5 %collective-permute-start.2 = (bf16[832,128]{1,0:T(8,128)(2,1)S(1)}, bf16[832,128]{1,0:T(8,128)(2,1)S(1)}, u32[]{:S(2)}, u32[]{:S(2)}) collective-permute-start(bf16[832,128]{1,0:T(8,128)(2,1)S(1)} %get-tuple-element.25), channel_id=1, source_target_pairs={{0,12},{1,13},{2,14},{3,15},{4,0},{5,1},{6,2},{7,3},{8,4},{9,5},{1... | collective-permute-start | bytes 638984 | tf_op jit(solution)/shard_map/ppermute | solution.py:292
  35.7 2.5 %all-to-all-done = bf16[64,16,256]{2,1,0:T(8,128)(2,1)S(1)} async-done(((bf16[64,16,256]{2,1,0:T(8,128)(2,1)}), bf16[64,16,256]{2,1,0:T(8,128)(2,1)S(1)}, u32[]{:S(2)}, u32[]{:S(2)}) %all-to-all-start) | async-done | bytes 524320 | tf_op jit(solution)/shard_map/all_to_all | solution.py:301
  38.2 1.9 %collective-permute-start.8 = (bf16[8,128,256]{2,1,0:T(8,128)(2,1)S(1)}, bf16[8,128,256]{2,1,0:T(8,128)(2,1)S(1)}, u32[]{:S(2)}, u32[]{:S(2)}) collective-permute-start(bf16[8,128,256]{2,1,0:T(8,128)(2,1)S(1)} %bitcast.21), channel_id=1, source_target_pairs={{0,1},{1,0},{2,3},{3,2},{4,5},{5,4},{6,7},{7,6},{8,9},{9,8},{10,11... | collective-permute-start | bytes 1572872 | tf_op jit(solution)/shard_map/ppermute | solution.py:307
  40.1 1.3 %collective-permute-start.3 = (bf16[8,128,256]{2,1,0:T(8,128)(2,1)S(1)}, bf16[8,128,256]{2,1,0:T(8,128)(2,1)S(1)}, u32[]{:S(2)}, u32[]{:S(2)}) collective-permute-start(bf16[8,128,256]{2,1,0:T(8,128)(2,1)S(1)} %bitcast.22), channel_id=1, source_target_pairs={{0,128},{1,129},{2,130},{3,131},{4,132},{5,133},{6,134},{7,135},{8... | collective-permute-start | bytes 1572872 | tf_op jit(solution)/shard_map/ppermute | solution.py:336
  41.4 1.2 collective-permute-done
  42.6 1.3 %collective-permute-start.4 = (bf16[8,128,256]{2,1,0:T(8,128)(2,1)S(1)}, bf16[8,128,256]{2,1,0:T(8,128)(2,1)S(1)}, u32[]{:S(2)}, u32[]{:S(2)}) collective-permute-start(bf16[8,128,256]{2,1,0:T(8,128)(2,1)S(1)} %bitcast.23), channel_id=1, source_target_pairs={{0,384},{1,385},{2,386},{3,387},{4,388},{5,389},{6,390},{7,391},{8... | collective-permute-start | bytes 1572872 | tf_op jit(solution)/shard_map/ppermute | solution.py:336
  43.9 10.3 %collective-permute-done.1 = bf16[832,128]{1,0:T(8,128)(2,1)S(1)} collective-permute-done((bf16[832,128]{1,0:T(8,128)(2,1)S(1)}, bf16[832,128]{1,0:T(8,128)(2,1)S(1)}, u32[]{:S(2)}, u32[]{:S(2)}) %collective-permute-start.1) | collective-permute-done | bytes 213024 | tf_op jit(solution)/shard_map/ppermute | solution.py:292
  54.2 1.3 %collective-permute-start.5 = (bf16[8,128,256]{2,1,0:T(8,128)(2,1)S(1)}, bf16[8,128,256]{2,1,0:T(8,128)(2,1)S(1)}, u32[]{:S(2)}, u32[]{:S(2)}) collective-permute-start(bf16[8,128,256]{2,1,0:T(8,128)(2,1)S(1)} %bitcast.24), channel_id=1, source_target_pairs={{0,256},{1,257},{2,258},{3,259},{4,260},{5,261},{6,262},{7,263},{8... | collective-permute-start | bytes 1572872 | tf_op jit(solution)/shard_map/ppermute | solution.py:336
  55.6 1.9 %collective-permute-start.7 = (bf16[4,256,128]{2,1,0:T(8,128)(2,1)S(1)}, bf16[4,256,128]{2,1,0:T(8,128)(2,1)S(1)}, u32[]{:S(2)}, u32[]{:S(2)}) collective-permute-start(bf16[4,256,128]{2,1,0:T(8,128)(2,1)S(1)} %pad_maximum_fusion.1.kv_o), channel_id=1, source_target_pairs={{0,2},{1,3},{2,0},{3,1},{4,6},{5,7},{6,4},{7,5},{8,10},{9,11},{10,... | collective-permute-start | bytes 786440 | tf_op jit(solution)/shard_map/ppermute | solution.py:324
  57.7 1.9 %collective-permute-start.6 = (bf16[4,256,128]{2,1,0:T(8,128)(2,1)S(1)}, bf16[4,256,128]{2,1,0:T(8,128)(2,1)S(1)}, u32[]{:S(2)}, u32[]{:S(2)}) collective-permute-start(bf16[4,256,128]{2,1,0:T(8,128)(2,1)S(1)} %pad_maximum_fusion.1.kv_o), channel_id=1, source_target_pairs={{0,1},{1,0},{2,3},{3,2},{4,5},{5,4},{6,7},{7,6},{8,9},{9,8},{10,11... | collective-permute-start | bytes 786440 | tf_op jit(solution)/shard_map/ppermute | solution.py:325
  59.7 5.8 %attend_own_x.1 = (f32[4,576,128]{2,1,0:T(8,128)S(1)}, f32[4,576,128]{2,1,0:T(8,128)S(1)}, f32[4,576,128]{2,1,0:T(8,128)S(1)}) custom-call(s32[4]{0:T(128)S(1)} %pad_add_fusion.place, s32[32,32]{1,0:T(8,128)S(1)} %copy-done.1, bf16[4,576,128]{2,1,0:T(8,128)(2,1)S(1)} %pad_maximum_fusion.q_ref, bf16[8,128,256]{2,1,0:T(8,128)(2,1)S(1)} %bitcast.25, ...), custom_call_target="tpu_custom_call" | custom-call | flops 1000 | bytes 1000 | tf_op jit(solution)/shard_map/attend_own_x/pallas_call | solution.py:315
  65.6 2.3 %collective-permute-start.9 = (bf16[4,256,128]{2,1,0:T(8,128)(2,1)S(1)}, bf16[4,256,128]{2,1,0:T(8,128)(2,1)S(1)}, u32[]{:S(2)}, u32[]{:S(2)}) collective-permute-start(bf16[4,256,128]{2,1,0:T(8,128)(2,1)S(1)} %collective-permute-done.7.kv_z), channel_id=1, source_target_pairs={{0,1},{1,0},{2,3},{3,2},{4,5},{5,4},{6,7},{7,6},{8,9},{9,8},{10,11... | collective-permute-start | bytes 786440 | tf_op jit(solution)/shard_map/ppermute | solution.py:327
  67.9 1.1 collective-permute-done.9.kv_zc
  69.1 5.9 %attend_raw.1 = (f32[4,576,128]{2,1,0:T(8,128)S(1)}, f32[4,576,128]{2,1,0:T(8,128)S(1)}, f32[4,576,128]{2,1,0:T(8,128)S(1)}) custom-call(s32[4]{0:T(128)S(1)} %pad_add_fusion.place, s32[256,128]{1,0:T(8,128)S(1)} %broadcast_in_dim.2.bpos, bf16[4,576,128]{2,1,0:T(8,128)(2,1)S(1)} %pad_maximum_fusion.q_ref, bf16[4,256,128]{2,1,0:T(8,128)(2,1)S(1)} %pad_maximum_fusion.1.kv_o, ...), custom_call_target="tpu_custom_call" | custom-call | flops 1000 | bytes 1000 | tf_op jit(solution)/shard_map/attend_raw/pallas_call | solution.py:328
  75.1 2.3 %collective-permute-start.10 = (bf16[8,128,256]{2,1,0:T(8,128)(2,1)S(1)}, bf16[8,128,256]{2,1,0:T(8,128)(2,1)S(1)}, u32[]{:S(2)}, u32[]{:S(2)}) collective-permute-start(bf16[8,128,256]{2,1,0:T(8,128)(2,1)S(1)} %collective-permute-done.3.rest_0_), channel_id=1, source_target_pairs={{0,1},{1,0},{2,3},{3,2},{4,5},{5,4},{6,7},{7,6},{8,9},{9,8},{10,11... | collective-permute-start | bytes 1572872 | tf_op jit(solution)/shard_map/ppermute | solution.py:338
  77.4 2.0 %collective-permute-start.11 = (bf16[8,128,256]{2,1,0:T(8,128)(2,1)S(1)}, bf16[8,128,256]{2,1,0:T(8,128)(2,1)S(1)}, u32[]{:S(2)}, u32[]{:S(2)}) collective-permute-start(bf16[8,128,256]{2,1,0:T(8,128)(2,1)S(1)} %collective-permute-done.4.rest_1_), channel_id=1, source_target_pairs={{0,1},{1,0},{2,3},{3,2},{4,5},{5,4},{6,7},{7,6},{8,9},{9,8},{10,11... | collective-permute-start | bytes 1572872 | tf_op jit(solution)/shard_map/ppermute | solution.py:338
  79.5 2.3 %collective-permute-start.12 = (bf16[8,128,256]{2,1,0:T(8,128)(2,1)S(1)}, bf16[8,128,256]{2,1,0:T(8,128)(2,1)S(1)}, u32[]{:S(2)}, u32[]{:S(2)}) collective-permute-start(bf16[8,128,256]{2,1,0:T(8,128)(2,1)S(1)} %collective-permute-done.5.rest_2_), channel_id=1, source_target_pairs={{0,1},{1,0},{2,3},{3,2},{4,5},{5,4},{6,7},{7,6},{8,9},{9,8},{10,11... | collective-permute-start | bytes 1572872 | tf_op jit(solution)/shard_map/ppermute | solution.py:338
  81.8 1.5 %collective-permute-done.12.rest_5_ = bf16[8,128,256]{2,1,0:T(8,128)(2,1)S(1)} collective-permute-done((bf16[8,128,256]{2,1,0:T(8,128)(2,1)S(1)}, bf16[8,128,256]{2,1,0:T(8,128)(2,1)S(1)}, u32[]{:S(2)}, u32[]{:S(2)}) %collective-permute-start.12) | collective-permute-done | bytes 524320 | tf_op jit(solution)/shard_map/ppermute | solution.py:338
  83.3 13.6 %attend_prior_2.1 = (bf16[576,128]{1,0:T(8,128)(2,1)S(1)}, bf16[576,128]{1,0:T(8,128)(2,1)S(1)}) custom-call(s32[4]{0:T(128)S(1)} %pad_add_fusion.place, s32[32,32]{1,0:T(8,128)S(1)} %copy-done.1, bf16[4,576,128]{2,1,0:T(8,128)(2,1)S(1)} %pad_maximum_fusion.q_ref, bf16[8,128,256]{2,1,0:T(8,128)(2,1)S(1)} %collective-permute-done.3.rest_0_, ...), custom_call_target="tpu_custom_call" | custom-call | flops 1000 | bytes 1000 | tf_op jit(solution)/shard_map/attend_prior_2/pallas_call | solution.py:342
  96.9 5.8 %collective-permute-start.14 = (bf16[576,128]{1,0:T(8,128)(2,1)S(1)}, bf16[576,128]{1,0:T(8,128)(2,1)S(1)}, u32[]{:S(2)}, u32[]{:S(2)}) collective-permute-start(bf16[576,128]{1,0:T(8,128)(2,1)S(1)} %get-tuple-element.40), channel_id=1, source_target_pairs={{0,8},{1,9},{2,10},{3,11},{4,12},{5,13},{6,14},{7,15},{8,0},{9,1},... | collective-permute-start | bytes 442376 | tf_op jit(solution)/shard_map/ppermute | solution.py:353
  102.7 1.9 %collective-permute-start.15 = (bf16[576,128]{1,0:T(8,128)(2,1)S(1)}, bf16[576,128]{1,0:T(8,128)(2,1)S(1)}, u32[]{:S(2)}, u32[]{:S(2)}) collective-permute-start(bf16[576,128]{1,0:T(8,128)(2,1)S(1)} %get-tuple-element.41), channel_id=1, source_target_pairs={{0,4},{1,5},{2,6},{3,7},{4,8},{5,9},{6,10},{7,11},{8,12},{9,13},{1... | collective-permute-start | bytes 442376 | tf_op jit(solution)/shard_map/ppermute | solution.py:353
  104.6 7.8 %attend_prior_1.1 = bf16[576,128]{1,0:T(8,128)(2,1)S(1)} custom-call(s32[4]{0:T(128)S(1)} %pad_add_fusion.place, s32[32,32]{1,0:T(8,128)S(1)} %copy-done.1, bf16[4,576,128]{2,1,0:T(8,128)(2,1)S(1)} %pad_maximum_fusion.q_ref, bf16[8,128,256]{2,1,0:T(8,128)(2,1)S(1)} %collective-permute-done.3.rest_0_, ...), custom_call_target="tpu_custom_call" | custom-call | flops 1000 | bytes 1000 | tf_op jit(solution)/shard_map/attend_prior_1/pallas_call | solution.py:342
  112.4 6.0 %collective-permute-start.13 = (bf16[576,128]{1,0:T(8,128)(2,1)S(1)}, bf16[576,128]{1,0:T(8,128)(2,1)S(1)}, u32[]{:S(2)}, u32[]{:S(2)}) collective-permute-start(bf16[576,128]{1,0:T(8,128)(2,1)S(1)} %attend_prior_1.1), channel_id=1, source_target_pairs={{0,12},{1,13},{2,14},{3,15},{4,0},{5,1},{6,2},{7,3},{8,4},{9,5},{1... | collective-permute-start | bytes 442376 | tf_op jit(solution)/shard_map/ppermute | solution.py:353
  118.5 7.8 %attend_prior_0.1.r0 = bf16[576,128]{1,0:T(8,128)(2,1)S(1)} custom-call(s32[4]{0:T(128)S(1)} %pad_add_fusion.place, s32[32,32]{1,0:T(8,128)S(1)} %copy-done.1, bf16[4,576,128]{2,1,0:T(8,128)(2,1)S(1)} %pad_maximum_fusion.q_ref, bf16[8,128,256]{2,1,0:T(8,128)(2,1)S(1)} %collective-permute-done.3.rest_0_, ...), custom_call_target="tpu_custom_call" | custom-call | flops 1000 | bytes 1000 | tf_op jit(solution)/shard_map/attend_prior_0/pallas_call | solution.py:342
  126.3 1.5 %unpack_outputs.1 = (bf16[128,2048]{1,0:T(8,128)(2,1)}, bf16[16,2048]{1,0:T(8,128)(2,1)}) custom-call(s32[4]{0:T(128)S(1)} %pad_add_fusion.place, bf16[576,128]{1,0:T(8,128)(2,1)S(1)} %attend_prior_0.1.r0, bf16[576,128]{1,0:T(8,128)(2,1)S(1)} %collective-permute-done.13.r1, bf16[576,128]{1,0:T(8,128)(2,1)S(1)} %collective-permute-done.14.r2, ...), custom_call_target="tpu_custom_call" | custom-call | bytes 1000 | tf_op jit(solution)/shard_map/unpack_outputs/pallas_call | solution.py:355
  (34 shorter events, 0.5 us)
Async XLA Ops:
  0.6 19.1 %copy-start.3 = (bf16[128,512]{1,0:T(8,128)(2,1)S(1)}, bf16[128,512]{1,0:T(8,128)(2,1)}, u32[]{:S(2)}) copy-start(bf16[128,512]{1,0:T(8,128)(2,1)} %v_ref.2) | copy-start | bytes 393220
  0.6 19.1 %copy-start.4 = (bf16[16,2048]{1,0:T(8,128)(2,1)S(1)}, bf16[16,2048]{1,0:T(8,128)(2,1)}, u32[]{:S(2)}) copy-start(bf16[16,2048]{1,0:T(8,128)(2,1)} %bq_ref.1) | copy-start | bytes 196612
  0.7 19.0 %copy-start = (bf16[128,2048]{1,0:T(8,128)(2,1)S(1)}, bf16[128,2048]{1,0:T(8,128)(2,1)}, u32[]{:S(2)}) copy-start(bf16[128,2048]{1,0:T(8,128)(2,1)} %q_ref.1) | copy-start | bytes 1572868
  0.7 19.0 %copy-start.2 = (bf16[128,512]{1,0:T(8,128)(2,1)S(1)}, bf16[128,512]{1,0:T(8,128)(2,1)}, u32[]{:S(2)}) copy-start(bf16[128,512]{1,0:T(8,128)(2,1)} %k_ref.2) | copy-start | bytes 393220
  0.7 0.8 copy-start.5
  1.5 0.7 copy-start.6
  3.0 35.2 %all-to-all-start = ((bf16[64,16,256]{2,1,0:T(8,128)(2,1)}), bf16[64,16,256]{2,1,0:T(8,128)(2,1)S(1)}, u32[]{:S(2)}, u32[]{:S(2)}) async-start(bf16[64,16,256]{2,1,0:T(8,128)(2,1)} %pack_beacons.1), calls=%async_computation | async-start | bytes 1048576 | tf_op jit(solution)/shard_map/all_to_all | solution.py:301
  20.5 22.2 %collective-permute-start = (bf16[832,128]{1,0:T(8,128)(2,1)S(1)}, bf16[832,128]{1,0:T(8,128)(2,1)S(1)}, u32[]{:S(2)}, u32[]{:S(2)}) collective-permute-start(bf16[832,128]{1,0:T(8,128)(2,1)S(1)} %get-tuple-element.23), channel_id=1, source_target_pairs={{0,4},{1,5},{2,6},{3,7},{4,8},{5,9},{6,10},{7,11},{8,12},{9,13},{1... | collective-permute-start | bytes 638984 | tf_op jit(solution)/shard_map/ppermute | solution.py:292
  24.7 29.5 %collective-permute-start.1 = (bf16[832,128]{1,0:T(8,128)(2,1)S(1)}, bf16[832,128]{1,0:T(8,128)(2,1)S(1)}, u32[]{:S(2)}, u32[]{:S(2)}) collective-permute-start(bf16[832,128]{1,0:T(8,128)(2,1)S(1)} %get-tuple-element.24), channel_id=1, source_target_pairs={{0,8},{1,9},{2,10},{3,11},{4,12},{5,13},{6,14},{7,15},{8,0},{9,1},... | collective-permute-start | bytes 638984 | tf_op jit(solution)/shard_map/ppermute | solution.py:292
  30.2 25.3 %collective-permute-start.2 = (bf16[832,128]{1,0:T(8,128)(2,1)S(1)}, bf16[832,128]{1,0:T(8,128)(2,1)S(1)}, u32[]{:S(2)}, u32[]{:S(2)}) collective-permute-start(bf16[832,128]{1,0:T(8,128)(2,1)S(1)} %get-tuple-element.25), channel_id=1, source_target_pairs={{0,12},{1,13},{2,14},{3,15},{4,0},{5,1},{6,2},{7,3},{8,4},{9,5},{1... | collective-permute-start | bytes 638984 | tf_op jit(solution)/shard_map/ppermute | solution.py:292
  38.2 19.5 %collective-permute-start.8 = (bf16[8,128,256]{2,1,0:T(8,128)(2,1)S(1)}, bf16[8,128,256]{2,1,0:T(8,128)(2,1)S(1)}, u32[]{:S(2)}, u32[]{:S(2)}) collective-permute-start(bf16[8,128,256]{2,1,0:T(8,128)(2,1)S(1)} %bitcast.21), channel_id=1, source_target_pairs={{0,1},{1,0},{2,3},{3,2},{4,5},{5,4},{6,7},{7,6},{8,9},{9,8},{10,11... | collective-permute-start | bytes 1572872 | tf_op jit(solution)/shard_map/ppermute | solution.py:307
  40.1 35.0 %collective-permute-start.3 = (bf16[8,128,256]{2,1,0:T(8,128)(2,1)S(1)}, bf16[8,128,256]{2,1,0:T(8,128)(2,1)S(1)}, u32[]{:S(2)}, u32[]{:S(2)}) collective-permute-start(bf16[8,128,256]{2,1,0:T(8,128)(2,1)S(1)} %bitcast.22), channel_id=1, source_target_pairs={{0,128},{1,129},{2,130},{3,131},{4,132},{5,133},{6,134},{7,135},{8... | collective-permute-start | bytes 1572872 | tf_op jit(solution)/shard_map/ppermute | solution.py:336
  42.6 32.5 %collective-permute-start.4 = (bf16[8,128,256]{2,1,0:T(8,128)(2,1)S(1)}, bf16[8,128,256]{2,1,0:T(8,128)(2,1)S(1)}, u32[]{:S(2)}, u32[]{:S(2)}) collective-permute-start(bf16[8,128,256]{2,1,0:T(8,128)(2,1)S(1)} %bitcast.23), channel_id=1, source_target_pairs={{0,384},{1,385},{2,386},{3,387},{4,388},{5,389},{6,390},{7,391},{8... | collective-permute-start | bytes 1572872 | tf_op jit(solution)/shard_map/ppermute | solution.py:336
  54.2 20.9 %collective-permute-start.5 = (bf16[8,128,256]{2,1,0:T(8,128)(2,1)S(1)}, bf16[8,128,256]{2,1,0:T(8,128)(2,1)S(1)}, u32[]{:S(2)}, u32[]{:S(2)}) collective-permute-start(bf16[8,128,256]{2,1,0:T(8,128)(2,1)S(1)} %bitcast.24), channel_id=1, source_target_pairs={{0,256},{1,257},{2,258},{3,259},{4,260},{5,261},{6,262},{7,263},{8... | collective-permute-start | bytes 1572872 | tf_op jit(solution)/shard_map/ppermute | solution.py:336
  55.6 4.0 %copy-start.1 = (s32[32,32]{1,0:T(8,128)S(1)}, s32[32,32]{1,0:T(8,128)}, u32[]{:S(2)}) copy-start(s32[32,32]{1,0:T(8,128)} %visible.7) | copy-start | bytes 12292
  55.6 10.0 %collective-permute-start.7 = (bf16[4,256,128]{2,1,0:T(8,128)(2,1)S(1)}, bf16[4,256,128]{2,1,0:T(8,128)(2,1)S(1)}, u32[]{:S(2)}, u32[]{:S(2)}) collective-permute-start(bf16[4,256,128]{2,1,0:T(8,128)(2,1)S(1)} %pad_maximum_fusion.1.kv_o), channel_id=1, source_target_pairs={{0,2},{1,3},{2,0},{3,1},{4,6},{5,7},{6,4},{7,5},{8,10},{9,11},{10,... | collective-permute-start | bytes 786440 | tf_op jit(solution)/shard_map/ppermute | solution.py:324
  57.6 11.4 %copy-start.7 = (s32[256]{0:T(256)S(1)}, s32[256]{0:T(256)}, u32[]{:S(2)}) copy-start(s32[256]{0:T(256)} %param.14) | copy-start | bytes 3076
  57.7 10.2 %collective-permute-start.6 = (bf16[4,256,128]{2,1,0:T(8,128)(2,1)S(1)}, bf16[4,256,128]{2,1,0:T(8,128)(2,1)S(1)}, u32[]{:S(2)}, u32[]{:S(2)}) collective-permute-start(bf16[4,256,128]{2,1,0:T(8,128)(2,1)S(1)} %pad_maximum_fusion.1.kv_o), channel_id=1, source_target_pairs={{0,1},{1,0},{2,3},{3,2},{4,5},{5,4},{6,7},{7,6},{8,9},{9,8},{10,11... | collective-permute-start | bytes 786440 | tf_op jit(solution)/shard_map/ppermute | solution.py:325
  65.6 3.5 %collective-permute-start.9 = (bf16[4,256,128]{2,1,0:T(8,128)(2,1)S(1)}, bf16[4,256,128]{2,1,0:T(8,128)(2,1)S(1)}, u32[]{:S(2)}, u32[]{:S(2)}) collective-permute-start(bf16[4,256,128]{2,1,0:T(8,128)(2,1)S(1)} %collective-permute-done.7.kv_z), channel_id=1, source_target_pairs={{0,1},{1,0},{2,3},{3,2},{4,5},{5,4},{6,7},{7,6},{8,9},{9,8},{10,11... | collective-permute-start | bytes 786440 | tf_op jit(solution)/shard_map/ppermute | solution.py:327
  75.1 6.6 %collective-permute-start.10 = (bf16[8,128,256]{2,1,0:T(8,128)(2,1)S(1)}, bf16[8,128,256]{2,1,0:T(8,128)(2,1)S(1)}, u32[]{:S(2)}, u32[]{:S(2)}) collective-permute-start(bf16[8,128,256]{2,1,0:T(8,128)(2,1)S(1)} %collective-permute-done.3.rest_0_), channel_id=1, source_target_pairs={{0,1},{1,0},{2,3},{3,2},{4,5},{5,4},{6,7},{7,6},{8,9},{9,8},{10,11... | collective-permute-start | bytes 1572872 | tf_op jit(solution)/shard_map/ppermute | solution.py:338
  77.4 4.4 %collective-permute-start.11 = (bf16[8,128,256]{2,1,0:T(8,128)(2,1)S(1)}, bf16[8,128,256]{2,1,0:T(8,128)(2,1)S(1)}, u32[]{:S(2)}, u32[]{:S(2)}) collective-permute-start(bf16[8,128,256]{2,1,0:T(8,128)(2,1)S(1)} %collective-permute-done.4.rest_1_), channel_id=1, source_target_pairs={{0,1},{1,0},{2,3},{3,2},{4,5},{5,4},{6,7},{7,6},{8,9},{9,8},{10,11... | collective-permute-start | bytes 1572872 | tf_op jit(solution)/shard_map/ppermute | solution.py:338
  79.5 3.8 %collective-permute-start.12 = (bf16[8,128,256]{2,1,0:T(8,128)(2,1)S(1)}, bf16[8,128,256]{2,1,0:T(8,128)(2,1)S(1)}, u32[]{:S(2)}, u32[]{:S(2)}) collective-permute-start(bf16[8,128,256]{2,1,0:T(8,128)(2,1)S(1)} %collective-permute-done.5.rest_2_), channel_id=1, source_target_pairs={{0,1},{1,0},{2,3},{3,2},{4,5},{5,4},{6,7},{7,6},{8,9},{9,8},{10,11... | collective-permute-start | bytes 1572872 | tf_op jit(solution)/shard_map/ppermute | solution.py:338
  96.9 29.4 %collective-permute-start.14 = (bf16[576,128]{1,0:T(8,128)(2,1)S(1)}, bf16[576,128]{1,0:T(8,128)(2,1)S(1)}, u32[]{:S(2)}, u32[]{:S(2)}) collective-permute-start(bf16[576,128]{1,0:T(8,128)(2,1)S(1)} %get-tuple-element.40), channel_id=1, source_target_pairs={{0,8},{1,9},{2,10},{3,11},{4,12},{5,13},{6,14},{7,15},{8,0},{9,1},... | collective-permute-start | bytes 442376 | tf_op jit(solution)/shard_map/ppermute | solution.py:353
  102.7 23.6 %collective-permute-start.15 = (bf16[576,128]{1,0:T(8,128)(2,1)S(1)}, bf16[576,128]{1,0:T(8,128)(2,1)S(1)}, u32[]{:S(2)}, u32[]{:S(2)}) collective-permute-start(bf16[576,128]{1,0:T(8,128)(2,1)S(1)} %get-tuple-element.41), channel_id=1, source_target_pairs={{0,4},{1,5},{2,6},{3,7},{4,8},{5,9},{6,10},{7,11},{8,12},{9,13},{1... | collective-permute-start | bytes 442376 | tf_op jit(solution)/shard_map/ppermute | solution.py:353
  112.4 13.9 %collective-permute-start.13 = (bf16[576,128]{1,0:T(8,128)(2,1)S(1)}, bf16[576,128]{1,0:T(8,128)(2,1)S(1)}, u32[]{:S(2)}, u32[]{:S(2)}) collective-permute-start(bf16[576,128]{1,0:T(8,128)(2,1)S(1)} %attend_prior_1.1), channel_id=1, source_target_pairs={{0,12},{1,13},{2,14},{3,15},{4,0},{5,1},{6,2},{7,3},{8,4},{9,5},{1... | collective-permute-start | bytes 442376 | tf_op jit(solution)/shard_map/ppermute | solution.py:353

commit v3 on v1

--- a/solution.py
+++ b/solution.py
@@ -333,8 +333,11 @@
         flops=1000,
         byte_count=1000,
     )(place, bpos, asked, kv_o, kv_c, kv_z, kv_zc, block0, block0c, *state)
-    arriving = [lax.ppermute(block0, CHIPS, to_later_x(step)) for step in (1, 3, 2)]
-    *arriving, _ = lax.optimization_barrier((*arriving, state[1]))
+    near = [lax.ppermute(block0, CHIPS, to_later_x(step)) for step in (1, 3)]
+    *near, _ = lax.optimization_barrier((*near, kv_z))
+    far = lax.ppermute(block0, CHIPS, to_later_x(2))
+    far, _ = lax.optimization_barrier((far, state[1]))
+    arriving = [*near, far]
     crossed = [lax.ppermute(block, CHIPS, OTHER_CORE) for block in arriving]
     mixed = []
     for first, tiles in ((1, 3), (0, 1)):

time: 129 us -> 131 us (1.016)
  the two profiles are of different devices: /device:TPU:127 before, /device:TPU:54 now
where the time goes in v3:
time: 131 us; the launch traced here: 130 us
  starting transfers between devices  62.9 us (48%)
  Pallas kernels  43.4 us (33%)
  waiting for transfers between devices  21.1 us (16%)
  local copies, waits for them, and re-layouts  1.68 us (1%)
    pallas_call x2, Pallas kernels, on_device(): kernel_call(functools.partial(attend_prior, first), f'attend_prior_{first...  28.5 us
    all_to_all x1, starting transfers between devices, on_device(): arrived = lax.all_to_all(to_send, ('y', 'z'), 0, 0, tiled=True)  16.2 us
    ppermute x3, starting transfers between devices, on_device(): lax.ppermute(chunks[step], CHIPS, to_head_group(step))  15.3 us
    ppermute x3, starting transfers between devices, on_device(): lax.ppermute(mixed[step], CHIPS, to_head_group(-step))  13.2 us
    ppermute x3, waiting for transfers between devices, on_device(): lax.ppermute(chunks[step], CHIPS, to_head_group(step))  10.6 us
    ppermute x3, starting transfers between devices, on_device(): crossed = [lax.ppermute(block, CHIPS, OTHER_CORE) for block in arriving]  6.24 us
    pallas_call x1, Pallas kernels, on_device(): kernel_call(attend_raw, 'attend_raw', state_shape, [SMEM] + [VMEM] * 11,...  5.94 us
    pallas_call x1, Pallas kernels, on_device(): kernel_call(attend_own_x, 'attend_own_x', state_shape, [SMEM] * 2 + [VMEM...  5.85 us
  transfers between devices with their start and end apart: 17, of which 7 were waited for; matrix products, arithmetic and copies ran while one was open for 0% of the time, Pallas kernels for 16%

profile of v3, /device:TPU:54, one launch (start us, length us, event | category | flops | bytes accessed | tf_op | source)
XLA Modules:
  0.0 130.3 jit_solution(13166476294752699138)
XLA Ops:
  0.7 0.8 copy-done.5
  2.2 0.8 pack_beacons.1
  3.0 16.2 %all-to-all-start = ((bf16[64,16,256]{2,1,0:T(8,128)(2,1)}), bf16[64,16,256]{2,1,0:T(8,128)(2,1)S(1)}, u32[]{:S(2)}, u32[]{:S(2)}) async-start(bf16[64,16,256]{2,1,0:T(8,128)(2,1)} %pack_beacons.1), calls=%async_computation | async-start | bytes 1048576 | tf_op jit(solution)/shard_map/all_to_all | solution.py:301
  19.4 0.8 pack_tokens.1
  20.1 4.3 %collective-permute-start = (bf16[832,128]{1,0:T(8,128)(2,1)S(1)}, bf16[832,128]{1,0:T(8,128)(2,1)S(1)}, u32[]{:S(2)}, u32[]{:S(2)}) collective-permute-start(bf16[832,128]{1,0:T(8,128)(2,1)S(1)} %get-tuple-element.24), channel_id=1, source_target_pairs={{0,4},{1,5},{2,6},{3,7},{4,8},{5,9},{6,10},{7,11},{8,12},{9,13},{1... | collective-permute-start | bytes 638984 | tf_op jit(solution)/shard_map/ppermute | solution.py:292
  24.4 5.5 %collective-permute-start.1 = (bf16[832,128]{1,0:T(8,128)(2,1)S(1)}, bf16[832,128]{1,0:T(8,128)(2,1)S(1)}, u32[]{:S(2)}, u32[]{:S(2)}) collective-permute-start(bf16[832,128]{1,0:T(8,128)(2,1)S(1)} %get-tuple-element.25), channel_id=1, source_target_pairs={{0,8},{1,9},{2,10},{3,11},{4,12},{5,13},{6,14},{7,15},{8,0},{9,1},... | collective-permute-start | bytes 638984 | tf_op jit(solution)/shard_map/ppermute | solution.py:292
  29.9 5.5 %collective-permute-start.2 = (bf16[832,128]{1,0:T(8,128)(2,1)S(1)}, bf16[832,128]{1,0:T(8,128)(2,1)S(1)}, u32[]{:S(2)}, u32[]{:S(2)}) collective-permute-start(bf16[832,128]{1,0:T(8,128)(2,1)S(1)} %get-tuple-element.26), channel_id=1, source_target_pairs={{0,12},{1,13},{2,14},{3,15},{4,0},{5,1},{6,2},{7,3},{8,4},{9,5},{1... | collective-permute-start | bytes 638984 | tf_op jit(solution)/shard_map/ppermute | solution.py:292
  35.4 1.2 all-to-all-done
  36.6 1.9 %collective-permute-start.6 = (bf16[8,128,256]{2,1,0:T(8,128)(2,1)S(1)}, bf16[8,128,256]{2,1,0:T(8,128)(2,1)S(1)}, u32[]{:S(2)}, u32[]{:S(2)}) collective-permute-start(bf16[8,128,256]{2,1,0:T(8,128)(2,1)S(1)} %bitcast.21), channel_id=1, source_target_pairs={{0,1},{1,0},{2,3},{3,2},{4,5},{5,4},{6,7},{7,6},{8,9},{9,8},{10,11... | collective-permute-start | bytes 1572872 | tf_op jit(solution)/shard_map/ppermute | solution.py:307
  38.6 1.3 collective-permute-start.7
  39.9 2.1 %collective-permute-done = bf16[832,128]{1,0:T(8,128)(2,1)S(1)} collective-permute-done((bf16[832,128]{1,0:T(8,128)(2,1)S(1)}, bf16[832,128]{1,0:T(8,128)(2,1)S(1)}, u32[]{:S(2)}, u32[]{:S(2)}) %collective-permute-start) | collective-permute-done | bytes 213024 | tf_op jit(solution)/shard_map/ppermute | solution.py:292
  42.0 1.3 collective-permute-start.3
  43.3 8.5 %collective-permute-done.1 = bf16[832,128]{1,0:T(8,128)(2,1)S(1)} collective-permute-done((bf16[832,128]{1,0:T(8,128)(2,1)S(1)}, bf16[832,128]{1,0:T(8,128)(2,1)S(1)}, u32[]{:S(2)}, u32[]{:S(2)}) %collective-permute-start.1) | collective-permute-done | bytes 213024 | tf_op jit(solution)/shard_map/ppermute | solution.py:292
  51.8 1.3 collective-permute-start.4
  53.1 1.9 %collective-permute-start.5 = (bf16[4,256,128]{2,1,0:T(8,128)(2,1)S(1)}, bf16[4,256,128]{2,1,0:T(8,128)(2,1)S(1)}, u32[]{:S(2)}, u32[]{:S(2)}) collective-permute-start(bf16[4,256,128]{2,1,0:T(8,128)(2,1)S(1)} %pad_maximum_fusion.1.kv_o), channel_id=1, source_target_pairs={{0,2},{1,3},{2,0},{3,1},{4,6},{5,7},{6,4},{7,5},{8,10},{9,11},{10,... | collective-permute-start | bytes 786440 | tf_op jit(solution)/shard_map/ppermute | solution.py:324
  55.2 1.9 %collective-permute-start.8 = (bf16[4,256,128]{2,1,0:T(8,128)(2,1)S(1)}, bf16[4,256,128]{2,1,0:T(8,128)(2,1)S(1)}, u32[]{:S(2)}, u32[]{:S(2)}) collective-permute-start(bf16[4,256,128]{2,1,0:T(8,128)(2,1)S(1)} %pad_maximum_fusion.1.kv_o), channel_id=1, source_target_pairs={{0,1},{1,0},{2,3},{3,2},{4,5},{5,4},{6,7},{7,6},{8,9},{9,8},{10,11... | collective-permute-start | bytes 786440 | tf_op jit(solution)/shard_map/ppermute | solution.py:325
  57.2 5.8 %attend_own_x.1 = (f32[4,576,128]{2,1,0:T(8,128)S(1)}, f32[4,576,128]{2,1,0:T(8,128)S(1)}, f32[4,576,128]{2,1,0:T(8,128)S(1)}) custom-call(s32[4]{0:T(128)S(1)} %pad_add_fusion.place, s32[32,32]{1,0:T(8,128)S(1)} %copy-done.1, bf16[4,576,128]{2,1,0:T(8,128)(2,1)S(1)} %pad_maximum_fusion.q_ref, bf16[8,128,256]{2,1,0:T(8,128)(2,1)S(1)} %bitcast.25, ...), custom_call_target="tpu_custom_call" | custom-call | flops 1000 | bytes 1000 | tf_op jit(solution)/shard_map/attend_own_x/pallas_call | solution.py:315
  63.1 2.4 %collective-permute-start.9 = (bf16[4,256,128]{2,1,0:T(8,128)(2,1)S(1)}, bf16[4,256,128]{2,1,0:T(8,128)(2,1)S(1)}, u32[]{:S(2)}, u32[]{:S(2)}) collective-permute-start(bf16[4,256,128]{2,1,0:T(8,128)(2,1)S(1)} %collective-permute-done.5.kv_z), channel_id=1, source_target_pairs={{0,1},{1,0},{2,3},{3,2},{4,5},{5,4},{6,7},{7,6},{8,9},{9,8},{10,11... | collective-permute-start | bytes 786440 | tf_op jit(solution)/shard_map/ppermute | solution.py:327
  65.5 3.0 %collective-permute-done.4.rest_1_ = bf16[8,128,256]{2,1,0:T(8,128)(2,1)S(1)} collective-permute-done((bf16[8,128,256]{2,1,0:T(8,128)(2,1)S(1)}, bf16[8,128,256]{2,1,0:T(8,128)(2,1)S(1)}, u32[]{:S(2)}, u32[]{:S(2)}) %collective-permute-start.4) | collective-permute-done | bytes 524320 | tf_op jit(solution)/shard_map/ppermute | solution.py:336
  68.4 1.9 %collective-permute-start.10 = (bf16[8,128,256]{2,1,0:T(8,128)(2,1)S(1)}, bf16[8,128,256]{2,1,0:T(8,128)(2,1)S(1)}, u32[]{:S(2)}, u32[]{:S(2)}) collective-permute-start(bf16[8,128,256]{2,1,0:T(8,128)(2,1)S(1)} %collective-permute-done.3.rest_0_), channel_id=1, source_target_pairs={{0,1},{1,0},{2,3},{3,2},{4,5},{5,4},{6,7},{7,6},{8,9},{9,8},{10,11... | collective-permute-start | bytes 1572872 | tf_op jit(solution)/shard_map/ppermute | solution.py:341
  70.4 2.4 %collective-permute-start.11 = (bf16[8,128,256]{2,1,0:T(8,128)(2,1)S(1)}, bf16[8,128,256]{2,1,0:T(8,128)(2,1)S(1)}, u32[]{:S(2)}, u32[]{:S(2)}) collective-permute-start(bf16[8,128,256]{2,1,0:T(8,128)(2,1)S(1)} %collective-permute-done.4.rest_1_), channel_id=1, source_target_pairs={{0,1},{1,0},{2,3},{3,2},{4,5},{5,4},{6,7},{7,6},{8,9},{9,8},{10,11... | collective-permute-start | bytes 1572872 | tf_op jit(solution)/shard_map/ppermute | solution.py:341
  72.9 5.9 %attend_raw.1 = (f32[4,576,128]{2,1,0:T(8,128)S(1)}, f32[4,576,128]{2,1,0:T(8,128)S(1)}, f32[4,576,128]{2,1,0:T(8,128)S(1)}) custom-call(s32[4]{0:T(128)S(1)} %pad_add_fusion.place, s32[256,128]{1,0:T(8,128)S(1)} %broadcast_in_dim.2.bpos, bf16[4,576,128]{2,1,0:T(8,128)(2,1)S(1)} %pad_maximum_fusion.q_ref, bf16[4,256,128]{2,1,0:T(8,128)(2,1)S(1)} %pad_maximum_fusion.1.kv_o, ...), custom_call_target="tpu_custom_call" | custom-call | flops 1000 | bytes 1000 | tf_op jit(solution)/shard_map/attend_raw/pallas_call | solution.py:328
  78.9 1.9 %collective-permute-start.12 = (bf16[8,128,256]{2,1,0:T(8,128)(2,1)S(1)}, bf16[8,128,256]{2,1,0:T(8,128)(2,1)S(1)}, u32[]{:S(2)}, u32[]{:S(2)}) collective-permute-start(bf16[8,128,256]{2,1,0:T(8,128)(2,1)S(1)} %collective-permute-done.7.rest_2_), channel_id=1, source_target_pairs={{0,1},{1,0},{2,3},{3,2},{4,5},{5,4},{6,7},{7,6},{8,9},{9,8},{10,11... | collective-permute-start | bytes 1572872 | tf_op jit(solution)/shard_map/ppermute | solution.py:341
  80.8 1.9 %collective-permute-done.12.rest_5_ = bf16[8,128,256]{2,1,0:T(8,128)(2,1)S(1)} collective-permute-done((bf16[8,128,256]{2,1,0:T(8,128)(2,1)S(1)}, bf16[8,128,256]{2,1,0:T(8,128)(2,1)S(1)}, u32[]{:S(2)}, u32[]{:S(2)}) %collective-permute-start.12) | collective-permute-done | bytes 524320 | tf_op jit(solution)/shard_map/ppermute | solution.py:341
  82.7 20.3 %attend_prior_1.1 = (bf16[576,128]{1,0:T(8,128)(2,1)S(1)}, bf16[576,128]{1,0:T(8,128)(2,1)S(1)}, bf16[576,128]{1,0:T(8,128)(2,1)S(1)}) custom-call(s32[4]{0:T(128)S(1)} %pad_add_fusion.place, s32[32,32]{1,0:T(8,128)S(1)} %copy-done.1, bf16[4,576,128]{2,1,0:T(8,128)(2,1)S(1)} %pad_maximum_fusion.q_ref, ...), custom_call_target="tpu_custom_call" | custom-call | flops 1000 | bytes 1000 | tf_op jit(solution)/shard_map/attend_prior_1/pallas_call | solution.py:345
  103.0 5.2 %collective-permute-start.13 = (bf16[576,128]{1,0:T(8,128)(2,1)S(1)}, bf16[576,128]{1,0:T(8,128)(2,1)S(1)}, u32[]{:S(2)}, u32[]{:S(2)}) collective-permute-start(bf16[576,128]{1,0:T(8,128)(2,1)S(1)} %get-tuple-element.41), channel_id=1, source_target_pairs={{0,12},{1,13},{2,14},{3,15},{4,0},{5,1},{6,2},{7,3},{8,4},{9,5},{1... | collective-permute-start | bytes 442376 | tf_op jit(solution)/shard_map/ppermute | solution.py:356
  108.1 6.1 %collective-permute-start.14 = (bf16[576,128]{1,0:T(8,128)(2,1)S(1)}, bf16[576,128]{1,0:T(8,128)(2,1)S(1)}, u32[]{:S(2)}, u32[]{:S(2)}) collective-permute-start(bf16[576,128]{1,0:T(8,128)(2,1)S(1)} %get-tuple-element.42), channel_id=1, source_target_pairs={{0,8},{1,9},{2,10},{3,11},{4,12},{5,13},{6,14},{7,15},{8,0},{9,1},... | collective-permute-start | bytes 442376 | tf_op jit(solution)/shard_map/ppermute | solution.py:356
  114.3 1.9 %collective-permute-start.15 = (bf16[576,128]{1,0:T(8,128)(2,1)S(1)}, bf16[576,128]{1,0:T(8,128)(2,1)S(1)}, u32[]{:S(2)}, u32[]{:S(2)}) collective-permute-start(bf16[576,128]{1,0:T(8,128)(2,1)S(1)} %get-tuple-element.43), channel_id=1, source_target_pairs={{0,4},{1,5},{2,6},{3,7},{4,8},{5,9},{6,10},{7,11},{8,12},{9,13},{1... | collective-permute-start | bytes 442376 | tf_op jit(solution)/shard_map/ppermute | solution.py:356
  116.2 8.2 %attend_prior_0.1.r0 = bf16[576,128]{1,0:T(8,128)(2,1)S(1)} custom-call(s32[4]{0:T(128)S(1)} %pad_add_fusion.place, s32[32,32]{1,0:T(8,128)S(1)} %copy-done.1, bf16[4,576,128]{2,1,0:T(8,128)(2,1)S(1)} %pad_maximum_fusion.q_ref, bf16[8,128,256]{2,1,0:T(8,128)(2,1)S(1)} %collective-permute-done.3.rest_0_, ...), custom_call_target="tpu_custom_call" | custom-call | flops 1000 | bytes 1000 | tf_op jit(solution)/shard_map/attend_prior_0/pallas_call | solution.py:345
  124.4 1.4 %collective-permute-done.14.r2 = bf16[576,128]{1,0:T(8,128)(2,1)S(1)} collective-permute-done((bf16[576,128]{1,0:T(8,128)(2,1)S(1)}, bf16[576,128]{1,0:T(8,128)(2,1)S(1)}, u32[]{:S(2)}, u32[]{:S(2)}) %collective-permute-start.14) | collective-permute-done | bytes 147488 | tf_op jit(solution)/shard_map/ppermute | solution.py:356
  125.8 3.0 %collective-permute-done.15.r3 = bf16[576,128]{1,0:T(8,128)(2,1)S(1)} collective-permute-done((bf16[576,128]{1,0:T(8,128)(2,1)S(1)}, bf16[576,128]{1,0:T(8,128)(2,1)S(1)}, u32[]{:S(2)}, u32[]{:S(2)}) %collective-permute-start.15) | collective-permute-done | bytes 147488 | tf_op jit(solution)/shard_map/ppermute | solution.py:356
  128.8 1.5 %unpack_outputs.1 = (bf16[128,2048]{1,0:T(8,128)(2,1)}, bf16[16,2048]{1,0:T(8,128)(2,1)}) custom-call(s32[4]{0:T(128)S(1)} %pad_add_fusion.place, bf16[576,128]{1,0:T(8,128)(2,1)S(1)} %attend_prior_0.1.r0, bf16[576,128]{1,0:T(8,128)(2,1)S(1)} %collective-permute-done.13.r1, bf16[576,128]{1,0:T(8,128)(2,1)S(1)} %collective-permute-done.14.r2, ...), custom_call_target="tpu_custom_call" | custom-call | bytes 1000 | tf_op jit(solution)/shard_map/unpack_outputs/pallas_call | solution.py:358
  (33 shorter events, 1.1 us)
Async XLA Ops:
  0.6 18.7 %copy-start.3 = (bf16[128,512]{1,0:T(8,128)(2,1)S(1)}, bf16[128,512]{1,0:T(8,128)(2,1)}, u32[]{:S(2)}) copy-start(bf16[128,512]{1,0:T(8,128)(2,1)} %v_ref.2) | copy-start | bytes 393220
  0.6 18.7 %copy-start.4 = (bf16[16,2048]{1,0:T(8,128)(2,1)S(1)}, bf16[16,2048]{1,0:T(8,128)(2,1)}, u32[]{:S(2)}) copy-start(bf16[16,2048]{1,0:T(8,128)(2,1)} %bq_ref.1) | copy-start | bytes 196612
  0.7 18.7 %copy-start = (bf16[128,2048]{1,0:T(8,128)(2,1)S(1)}, bf16[128,2048]{1,0:T(8,128)(2,1)}, u32[]{:S(2)}) copy-start(bf16[128,2048]{1,0:T(8,128)(2,1)} %q_ref.1) | copy-start | bytes 1572868
  0.7 18.7 %copy-start.2 = (bf16[128,512]{1,0:T(8,128)(2,1)S(1)}, bf16[128,512]{1,0:T(8,128)(2,1)}, u32[]{:S(2)}) copy-start(bf16[128,512]{1,0:T(8,128)(2,1)} %k_ref.2) | copy-start | bytes 393220
  0.7 0.8 copy-start.5
  1.5 0.7 copy-start.6
  3.0 33.6 %all-to-all-start = ((bf16[64,16,256]{2,1,0:T(8,128)(2,1)}), bf16[64,16,256]{2,1,0:T(8,128)(2,1)S(1)}, u32[]{:S(2)}, u32[]{:S(2)}) async-start(bf16[64,16,256]{2,1,0:T(8,128)(2,1)} %pack_beacons.1), calls=%async_computation | async-start | bytes 1048576 | tf_op jit(solution)/shard_map/all_to_all | solution.py:301
  20.1 21.9 %collective-permute-start = (bf16[832,128]{1,0:T(8,128)(2,1)S(1)}, bf16[832,128]{1,0:T(8,128)(2,1)S(1)}, u32[]{:S(2)}, u32[]{:S(2)}) collective-permute-start(bf16[832,128]{1,0:T(8,128)(2,1)S(1)} %get-tuple-element.24), channel_id=1, source_target_pairs={{0,4},{1,5},{2,6},{3,7},{4,8},{5,9},{6,10},{7,11},{8,12},{9,13},{1... | collective-permute-start | bytes 638984 | tf_op jit(solution)/shard_map/ppermute | solution.py:292
  24.4 27.4 %collective-permute-start.1 = (bf16[832,128]{1,0:T(8,128)(2,1)S(1)}, bf16[832,128]{1,0:T(8,128)(2,1)S(1)}, u32[]{:S(2)}, u32[]{:S(2)}) collective-permute-start(bf16[832,128]{1,0:T(8,128)(2,1)S(1)} %get-tuple-element.25), channel_id=1, source_target_pairs={{0,8},{1,9},{2,10},{3,11},{4,12},{5,13},{6,14},{7,15},{8,0},{9,1},... | collective-permute-start | bytes 638984 | tf_op jit(solution)/shard_map/ppermute | solution.py:292
  29.9 23.1 %collective-permute-start.2 = (bf16[832,128]{1,0:T(8,128)(2,1)S(1)}, bf16[832,128]{1,0:T(8,128)(2,1)S(1)}, u32[]{:S(2)}, u32[]{:S(2)}) collective-permute-start(bf16[832,128]{1,0:T(8,128)(2,1)S(1)} %get-tuple-element.26), channel_id=1, source_target_pairs={{0,12},{1,13},{2,14},{3,15},{4,0},{5,1},{6,2},{7,3},{8,4},{9,5},{1... | collective-permute-start | bytes 638984 | tf_op jit(solution)/shard_map/ppermute | solution.py:292
  36.6 18.6 %collective-permute-start.6 = (bf16[8,128,256]{2,1,0:T(8,128)(2,1)S(1)}, bf16[8,128,256]{2,1,0:T(8,128)(2,1)S(1)}, u32[]{:S(2)}, u32[]{:S(2)}) collective-permute-start(bf16[8,128,256]{2,1,0:T(8,128)(2,1)S(1)} %bitcast.21), channel_id=1, source_target_pairs={{0,1},{1,0},{2,3},{3,2},{4,5},{5,4},{6,7},{7,6},{8,9},{9,8},{10,11... | collective-permute-start | bytes 1572872 | tf_op jit(solution)/shard_map/ppermute | solution.py:307
  38.6 40.3 %collective-permute-start.7 = (bf16[8,128,256]{2,1,0:T(8,128)(2,1)S(1)}, bf16[8,128,256]{2,1,0:T(8,128)(2,1)S(1)}, u32[]{:S(2)}, u32[]{:S(2)}) collective-permute-start(bf16[8,128,256]{2,1,0:T(8,128)(2,1)S(1)} %bitcast.22), channel_id=1, source_target_pairs={{0,256},{1,257},{2,258},{3,259},{4,260},{5,261},{6,262},{7,263},{8... | collective-permute-start | bytes 1572872 | tf_op jit(solution)/shard_map/ppermute | solution.py:338
  42.0 23.5 %collective-permute-start.3 = (bf16[8,128,256]{2,1,0:T(8,128)(2,1)S(1)}, bf16[8,128,256]{2,1,0:T(8,128)(2,1)S(1)}, u32[]{:S(2)}, u32[]{:S(2)}) collective-permute-start(bf16[8,128,256]{2,1,0:T(8,128)(2,1)S(1)} %bitcast.23), channel_id=1, source_target_pairs={{0,128},{1,129},{2,130},{3,131},{4,132},{5,133},{6,134},{7,135},{8... | collective-permute-start | bytes 1572872 | tf_op jit(solution)/shard_map/ppermute | solution.py:336
  51.8 16.7 %collective-permute-start.4 = (bf16[8,128,256]{2,1,0:T(8,128)(2,1)S(1)}, bf16[8,128,256]{2,1,0:T(8,128)(2,1)S(1)}, u32[]{:S(2)}, u32[]{:S(2)}) collective-permute-start(bf16[8,128,256]{2,1,0:T(8,128)(2,1)S(1)} %bitcast.24), channel_id=1, source_target_pairs={{0,384},{1,385},{2,386},{3,387},{4,388},{5,389},{6,390},{7,391},{8... | collective-permute-start | bytes 1572872 | tf_op jit(solution)/shard_map/ppermute | solution.py:336
  53.1 4.0 %copy-start.1 = (s32[32,32]{1,0:T(8,128)S(1)}, s32[32,32]{1,0:T(8,128)}, u32[]{:S(2)}) copy-start(s32[32,32]{1,0:T(8,128)} %visible.5) | copy-start | bytes 12292
  53.1 9.9 %collective-permute-start.5 = (bf16[4,256,128]{2,1,0:T(8,128)(2,1)S(1)}, bf16[4,256,128]{2,1,0:T(8,128)(2,1)S(1)}, u32[]{:S(2)}, u32[]{:S(2)}) collective-permute-start(bf16[4,256,128]{2,1,0:T(8,128)(2,1)S(1)} %pad_maximum_fusion.1.kv_o), channel_id=1, source_target_pairs={{0,2},{1,3},{2,0},{3,1},{4,6},{5,7},{6,4},{7,5},{8,10},{9,11},{10,... | collective-permute-start | bytes 786440 | tf_op jit(solution)/shard_map/ppermute | solution.py:324
  55.1 17.7 %copy-start.7 = (s32[256]{0:T(256)S(1)}, s32[256]{0:T(256)}, u32[]{:S(2)}) copy-start(s32[256]{0:T(256)} %param.14) | copy-start | bytes 3076
  55.2 17.5 %collective-permute-start.8 = (bf16[4,256,128]{2,1,0:T(8,128)(2,1)S(1)}, bf16[4,256,128]{2,1,0:T(8,128)(2,1)S(1)}, u32[]{:S(2)}, u32[]{:S(2)}) collective-permute-start(bf16[4,256,128]{2,1,0:T(8,128)(2,1)S(1)} %pad_maximum_fusion.1.kv_o), channel_id=1, source_target_pairs={{0,1},{1,0},{2,3},{3,2},{4,5},{5,4},{6,7},{7,6},{8,9},{9,8},{10,11... | collective-permute-start | bytes 786440 | tf_op jit(solution)/shard_map/ppermute | solution.py:325
  63.1 9.7 %collective-permute-start.9 = (bf16[4,256,128]{2,1,0:T(8,128)(2,1)S(1)}, bf16[4,256,128]{2,1,0:T(8,128)(2,1)S(1)}, u32[]{:S(2)}, u32[]{:S(2)}) collective-permute-start(bf16[4,256,128]{2,1,0:T(8,128)(2,1)S(1)} %collective-permute-done.5.kv_z), channel_id=1, source_target_pairs={{0,1},{1,0},{2,3},{3,2},{4,5},{5,4},{6,7},{7,6},{8,9},{9,8},{10,11... | collective-permute-start | bytes 786440 | tf_op jit(solution)/shard_map/ppermute | solution.py:327
  68.4 12.3 %collective-permute-start.10 = (bf16[8,128,256]{2,1,0:T(8,128)(2,1)S(1)}, bf16[8,128,256]{2,1,0:T(8,128)(2,1)S(1)}, u32[]{:S(2)}, u32[]{:S(2)}) collective-permute-start(bf16[8,128,256]{2,1,0:T(8,128)(2,1)S(1)} %collective-permute-done.3.rest_0_), channel_id=1, source_target_pairs={{0,1},{1,0},{2,3},{3,2},{4,5},{5,4},{6,7},{7,6},{8,9},{9,8},{10,11... | collective-permute-start | bytes 1572872 | tf_op jit(solution)/shard_map/ppermute | solution.py:341
  70.4 10.4 %collective-permute-start.11 = (bf16[8,128,256]{2,1,0:T(8,128)(2,1)S(1)}, bf16[8,128,256]{2,1,0:T(8,128)(2,1)S(1)}, u32[]{:S(2)}, u32[]{:S(2)}) collective-permute-start(bf16[8,128,256]{2,1,0:T(8,128)(2,1)S(1)} %collective-permute-done.4.rest_1_), channel_id=1, source_target_pairs={{0,1},{1,0},{2,3},{3,2},{4,5},{5,4},{6,7},{7,6},{8,9},{9,8},{10,11... | collective-permute-start | bytes 1572872 | tf_op jit(solution)/shard_map/ppermute | solution.py:341
  78.9 3.8 %collective-permute-start.12 = (bf16[8,128,256]{2,1,0:T(8,128)(2,1)S(1)}, bf16[8,128,256]{2,1,0:T(8,128)(2,1)S(1)}, u32[]{:S(2)}, u32[]{:S(2)}) collective-permute-start(bf16[8,128,256]{2,1,0:T(8,128)(2,1)S(1)} %collective-permute-done.7.rest_2_), channel_id=1, source_target_pairs={{0,1},{1,0},{2,3},{3,2},{4,5},{5,4},{6,7},{7,6},{8,9},{9,8},{10,11... | collective-permute-start | bytes 1572872 | tf_op jit(solution)/shard_map/ppermute | solution.py:341
  103.0 21.4 %collective-permute-start.13 = (bf16[576,128]{1,0:T(8,128)(2,1)S(1)}, bf16[576,128]{1,0:T(8,128)(2,1)S(1)}, u32[]{:S(2)}, u32[]{:S(2)}) collective-permute-start(bf16[576,128]{1,0:T(8,128)(2,1)S(1)} %get-tuple-element.41), channel_id=1, source_target_pairs={{0,12},{1,13},{2,14},{3,15},{4,0},{5,1},{6,2},{7,3},{8,4},{9,5},{1... | collective-permute-start | bytes 442376 | tf_op jit(solution)/shard_map/ppermute | solution.py:356
  108.1 17.7 %collective-permute-start.14 = (bf16[576,128]{1,0:T(8,128)(2,1)S(1)}, bf16[576,128]{1,0:T(8,128)(2,1)S(1)}, u32[]{:S(2)}, u32[]{:S(2)}) collective-permute-start(bf16[576,128]{1,0:T(8,128)(2,1)S(1)} %get-tuple-element.42), channel_id=1, source_target_pairs={{0,8},{1,9},{2,10},{3,11},{4,12},{5,13},{6,14},{7,15},{8,0},{9,1},... | collective-permute-start | bytes 442376 | tf_op jit(solution)/shard_map/ppermute | solution.py:356
  114.3 14.5 %collective-permute-start.15 = (bf16[576,128]{1,0:T(8,128)(2,1)S(1)}, bf16[576,128]{1,0:T(8,128)(2,1)S(1)}, u32[]{:S(2)}, u32[]{:S(2)}) collective-permute-start(bf16[576,128]{1,0:T(8,128)(2,1)S(1)} %get-tuple-element.43), channel_id=1, source_target_pairs={{0,4},{1,5},{2,6},{3,7},{4,8},{5,9},{6,10},{7,11},{8,12},{9,13},{1... | collective-permute-start | bytes 442376 | tf_op jit(solution)/shard_map/ppermute | solution.py:356
